TPU v7x, 32 devices: a whole 2x2x4 slice. The times are simulated.
32 devices in a mesh: outer: 2 (over x), inner: 16 (over z, y, core).
Axes of the slice: x: 2, y: 2, z: 4, core: 2. Of those that a mesh axis runs over, the one named last changes fastest.
Arguments:
- tokens: bfloat16 [8192, 2048], P(('outer', 'inner')), may hold values from -6 to 6
- w_qkv: bfloat16 [2048, 3072], P('inner'), may hold values from -2.8 to 2.8
- w_out: bfloat16 [1024, 2048], P(None, 'inner'), may hold values from -1.5 to 1.5
- neighbours: int32 [32, 5], P(('outer', 'inner')), may hold values from -1 to 31, as said below
- counts: int32 [32], replicated, may hold values from 1 to 256, as said below
Outputs:
- attended: bfloat16 [8192, 2048], P(('outer', 'inner'))
Inputs may be any that keep to these rules, and one draw needn't show every extreme that they name: `neighbours`: slot 0 of row b is b itself; slots 1 and 2 are the blocks b - 16 and b + 16 (the same inner index in the previous and next slab of outer), slots 3 and 4 the blocks b - 1 and b + 1 of the same slab; a slot holds -1 where its block lies outside the grid of blocks, and may hold -1 otherwise. `counts`: some block is full.
All inputs are finite; a program needn't handle non-finite values.
Results may differ from a plain program's by a relative error of at most 0.0093.
Values may be sent and summed in bfloat16 or wider, within the bound.
No kernel may reach another device: no remote copies, remote signals or barrier semaphores. Data moves between devices by JAX's collectives and lax.ppermute only.
A program may use at most 64 MiB of HBM per device.

v0:
```python
import jax
import jax.numpy as jnp
from jax import lax
from jax.sharding import PartitionSpec as P

HD = 128


def padded(block, sides, width):
    for axis, dim in sides:
        count = lax.axis_size(axis)
        forward = [(i, i + 1) for i in range(count - 1)]
        backward = [(target, source) for source, target in forward]
        low = lax.ppermute(
            lax.slice_in_dim(block, block.shape[dim] - width, None, axis=dim), axis, forward
        )
        high = lax.ppermute(lax.slice_in_dim(block, 0, width, axis=dim), axis, backward)
        block = jnp.concatenate([low, block, high], axis=dim)
    return block


def normalize(values_in):
    values = values_in.astype(jnp.float32)
    center = values - jnp.mean(values, axis=-1, keepdims=True)
    spread = jnp.mean(center * center, axis=-1, keepdims=True)
    return (center * lax.rsqrt(spread + 1e-05)).astype(jnp.bfloat16)


def per_device(tokens, w_qkv, w_out, neighbours, counts):
    normed = normalize(tokens)
    rows_here = normed.shape[0]
    heads_all = w_out.shape[0]
    head_size = HD
    projected = jnp.dot(
        normed,
        lax.all_gather(w_qkv, "inner", axis=0, tiled=True),
        preferred_element_type=jnp.float32,
    ).astype(jnp.bfloat16)
    queries = projected[:, :heads_all]
    keys_values = projected[:, heads_all:]
    slab_halo = padded(keys_values[None], (("outer", 0),), 1)
    row_halo = padded(keys_values[None], (("inner", 0),), 1)
    candidates = (keys_values, slab_halo[0], slab_halo[2], row_halo[0], row_halo[2])
    listed = neighbours[0]
    clipped = jnp.maximum(listed, 0)
    block_ids = jnp.arange(counts.shape[0], dtype=jnp.int32)
    lengths = jnp.sum(jnp.where(clipped[:, None] == block_ids[None, :], counts[None, :], 0), axis=1)
    positions = jnp.arange(rows_here, dtype=jnp.int32)
    usable = (listed[:, None] >= 0) & (positions[None, :] < lengths[:, None])
    allowed = usable.reshape(-1)
    score_scale = float(head_size) ** (-0.5)
    outputs = []
    for head_index in range(heads_all // head_size):
        offset_q = head_index * head_size
        offset_v = heads_all + offset_q
        query_head = queries[:, offset_q : offset_q + head_size]
        scores = (
            jnp.concatenate(
                [
                    jnp.einsum(
                        "qd,kd->qk",
                        query_head,
                        source_kv[:, offset_q : offset_q + head_size],
                        preferred_element_type=jnp.float32,
                    )
                    for source_kv in candidates
                ],
                axis=1,
            )
            * score_scale
        )
        masked = jnp.where(allowed[None, :], scores, -jnp.inf)
        largest = jnp.max(masked, axis=1, keepdims=True)
        weights = jnp.exp(masked - largest)
        totals = jnp.sum(weights, axis=1, keepdims=True)
        rounded = weights.astype(jnp.bfloat16)
        context = jnp.zeros((rows_here, head_size), jnp.float32)
        for slot_no in range(len(candidates)):
            context = context + jnp.dot(
                rounded[:, slot_no * rows_here : (slot_no + 1) * rows_here],
                candidates[slot_no][:, offset_v : offset_v + head_size],
                preferred_element_type=jnp.float32,
            )
        outputs.append((context / totals).astype(jnp.bfloat16))
    context_all = jnp.concatenate(outputs, axis=1)
    return jnp.dot(
        context_all,
        lax.all_gather(w_out, "inner", axis=1, tiled=True),
        preferred_element_type=jnp.float32,
    ).astype(jnp.bfloat16)


def solution(mesh):
    placed = (
        P(("outer", "inner"), None),
        P("inner", None),
        P(None, "inner"),
        P(("outer", "inner"), None),
        P(),
    )
    return jax.shard_map(
        per_device,
        mesh=mesh,
        in_specs=placed,
        out_specs=P(("outer", "inner"), None),
        check_vma=False,
    )
```

profile of v0, /device:TPU:19, one launch (start us, length us, event | category | flops | bytes accessed | tf_op | source)
XLA Modules:
  0.0 195.8 jit_solution(16174335047811111612)
XLA Ops:
  6.5 0.7 all-gather.3.cloned.1.call-update
  7.3 0.7 all-gather.5.cloned.1.call-update
  8.0 0.7 maximum_bitcast_fusion
  8.7 0.7 compare_bitcast_fusion
  9.6 0.4 fusion.2
  10.3 100.7 %all-gather.3.cloned.1.call-done = bf16[2048,3072]{1,0:T(8,128)(2,1)} async-done(((bf16[128,3072]{1,0:T(8,128)(2,1)}), bf16[2048,3072]{1,0:T(8,128)(2,1)}) %all-gather.3.cloned.1.call-update) | async-done | bytes 12582928 | tf_op jit(solution)/shard_map/all_gather | solution.py:36
  111.0 8.2 %convolution_convert_fusion = bf16[256,3072]{1,0:T(8,128)(2,1)S(1)} fusion(bf16[2048,3072]{1,0:T(8,128)(2,1)} %all-gather.3.cloned.1.call-done, bf16[256,2048]{1,0:T(8,128)(2,1)S(1)} %copy-done, f32[256]{0:T(256)S(1)} %add_rsqrt_fusion, f32[256]{0:T(256)S(1)} %broadcast_multiply_fusion), kind=kOutput, calls=%fused_computation | convolution fusion | flops 3224109056 | bytes 15206400 | tf_op jit(solution)/shard_map/dot_general | solution.py:34
  119.4 1.3 collective-permute-start
  120.7 4.1 %collective-permute-start.1 = (bf16[1,256,2048]{2,1,0:T(8,128)(2,1)S(1)}, bf16[1,256,2048]{2,1,0:T(8,128)(2,1)S(1)}, u32[]{:S(2)}, u32[]{:S(2)}) collective-permute-start(bf16[1,256,2048]{2,1,0:T(8,128)(2,1)S(1)} %slice_bitcast_fusion), channel_id=1, source_target_pairs={{16,0},{17,1},{18,2},{19,3},{20,4},{21,5},{22,6},{23,7},{24,8},{25... | collective-permute-start | bytes 3145736 | tf_op jit(solution)/shard_map/ppermute | solution.py:17
  124.9 2.9 %collective-permute-start.2 = (bf16[1,256,2048]{2,1,0:T(8,128)(2,1)S(1)}, bf16[1,256,2048]{2,1,0:T(8,128)(2,1)S(1)}, u32[]{:S(2)}, u32[]{:S(2)}) collective-permute-start(bf16[1,256,2048]{2,1,0:T(8,128)(2,1)S(1)} %slice_bitcast_fusion), channel_id=1, source_target_pairs={{0,1},{1,2},{2,3},{3,4},{4,5},{5,6},{6,7},{7,8},{8,9},{9,10},{10,1... | collective-permute-start | bytes 3145736 | tf_op jit(solution)/shard_map/ppermute | solution.py:14
  127.8 2.1 %collective-permute-start.3 = (bf16[1,256,2048]{2,1,0:T(8,128)(2,1)S(1)}, bf16[1,256,2048]{2,1,0:T(8,128)(2,1)S(1)}, u32[]{:S(2)}, u32[]{:S(2)}) collective-permute-start(bf16[1,256,2048]{2,1,0:T(8,128)(2,1)S(1)} %slice_bitcast_fusion), channel_id=1, source_target_pairs={{1,0},{2,1},{3,2},{4,3},{5,4},{6,5},{7,6},{8,7},{9,8},{10,9},{11,1... | collective-permute-start | bytes 3145736 | tf_op jit(solution)/shard_map/ppermute | solution.py:17
  131.2 14.8 %collective-permute-done = bf16[1,256,2048]{2,1,0:T(8,128)(2,1)S(1)} collective-permute-done((bf16[1,256,2048]{2,1,0:T(8,128)(2,1)S(1)}, bf16[1,256,2048]{2,1,0:T(8,128)(2,1)S(1)}, u32[]{:S(2)}, u32[]{:S(2)}) %collective-permute-start) | collective-permute-done | bytes 1048608 | tf_op jit(solution)/shard_map/ppermute | solution.py:14
  146.4 0.4 collective-permute-done.1
  147.2 14.5 %collective-permute-done.2 = bf16[1,256,2048]{2,1,0:T(8,128)(2,1)S(1)} collective-permute-done((bf16[1,256,2048]{2,1,0:T(8,128)(2,1)S(1)}, bf16[1,256,2048]{2,1,0:T(8,128)(2,1)S(1)}, u32[]{:S(2)}, u32[]{:S(2)}) %collective-permute-start.2) | collective-permute-done | bytes 1048608 | tf_op jit(solution)/shard_map/ppermute | solution.py:14
  162.0 3.5 %collective-permute-done.3 = bf16[1,256,2048]{2,1,0:T(8,128)(2,1)S(1)} collective-permute-done((bf16[1,256,2048]{2,1,0:T(8,128)(2,1)S(1)}, bf16[1,256,2048]{2,1,0:T(8,128)(2,1)S(1)}, u32[]{:S(2)}, u32[]{:S(2)}) %collective-permute-start.3) | collective-permute-done | bytes 1048608 | tf_op jit(solution)/shard_map/ppermute | solution.py:17
  170.5 0.4 fusion.11
  170.9 2.0 %fusion.69 = (f32[256]{0:T(256)S(1)}, f32[256]{0:T(256)S(1)}, f32[256]{0:T(256)S(1)}, f32[256]{0:T(256)S(1)}, f32[256]{0:T(256)S(1)}, /*index=5*/f32[256]{0:T(25...) fusion(f32[256,1280]{0,1:T(8,128)S(1)} %convolution_dynamic-update-slice_fusio, ...), kind=kLoop, calls=%fused_computation.145 | loop fusion | flops 9172992 | bytes 11808000 | tf_op jit(solution)/shard_map/reduce_sum | solution.py:75
  172.9 0.2 fusion.127
  173.1 0.2 fusion.129
  173.3 0.2 fusion.133
  173.6 2.3 %fusion.67 = (f32[256]{0:T(256)S(1)}, f32[256]{0:T(256)S(1)}, f32[256]{0:T(256)S(1)}, f32[256]{0:T(256)S(1)}, f32[256]{0:T(256)S(1)}, /*index=5*/f32[256]{0:T(25...) fusion(f32[256,1280]{0,1:T(8,128)S(1)} %convolution_dynamic-upd, ...), kind=kLoop, calls=%fused_computation.143 | loop fusion | flops 9828864 | bytes 11810048 | tf_op jit(solution)/shard_map/reduce_sum | solution.py:75
  175.8 0.2 fusion.119
  177.2 0.2 fusion.103
  177.4 0.2 fusion.105
  177.7 0.2 fusion.109
  177.9 0.2 fusion.95
  179.3 0.2 fusion.79
  179.5 0.2 fusion.81
  179.7 0.2 fusion.85
  180.0 0.2 fusion.71
  180.2 0.2 fusion.73
  180.7 0.2 convolution_add_fusion.15
  180.9 0.2 convolution_add_fusion.13
  181.1 0.2 convolution_add_fusion.11
  181.4 0.2 convolution_add_fusion.9
  181.6 0.2 convolution_add_fusion.7
  181.8 0.2 convolution_add_fusion.5
  182.0 0.2 convolution_add_fusion.3
  182.3 0.2 convolution_add_fusion.1
  182.5 0.2 fusion.51
  182.8 0.2 fusion.49
  183.0 0.2 fusion.47
  183.3 0.2 fusion.45
  183.5 0.2 fusion.43
  183.8 0.2 fusion.41
  184.0 0.2 fusion.39
  184.3 0.2 fusion.37
  184.6 4.4 %convolution_convert_fusion.1 = bf16[256,2048]{1,0:T(8,128)(2,1)} fusion(bf16[256,1024]{1,0:T(8,128)(2,1)S(1)} %fusion.37, bf16[1024,2048]{1,0:T(8,128)(2,1)} %all-gather.5.cloned.1.call-done), kind=kOutput, calls=%fused_computation.3 | convolution fusion | flops 1074266112 | bytes 5767168 | tf_op jit(solution)/shard_map/dot_general | solution.py:86
  (65 shorter events, 10.4 us)
Async XLA Ops:
  6.5 2.8 %copy-start = (bf16[256,2048]{1,0:T(8,128)(2,1)S(1)}, bf16[256,2048]{1,0:T(8,128)(2,1)}, u32[]{:S(2)}) copy-start(bf16[256,2048]{1,0:T(8,128)(2,1)} %param.5) | copy-start | bytes 3145732
  6.5 104.5 %all-gather.3.cloned.1.call-start = ((), (), s32[]{:S(2)}) async-start(), calls=%async_computation | async-start | bytes 13369344 | tf_op jit(solution)/shard_map/all_gather | solution.py:36
  7.3 2.7 %copy-start.1 = (s32[32]{0:T(128)S(1)}, s32[32]{0:T(128)}, u32[]{:S(2)}) copy-start(s32[32]{0:T(128)} %param.9) | copy-start | bytes 388
  7.3 177.3 %all-gather.5.cloned.1.call-start = ((), (), s32[]{:S(2)}) async-start(), calls=%async_computation.1 | async-start | bytes 4456448 | tf_op jit(solution)/shard_map/all_gather | solution.py:88
  119.4 26.5 %collective-permute-start = (bf16[1,256,2048]{2,1,0:T(8,128)(2,1)S(1)}, bf16[1,256,2048]{2,1,0:T(8,128)(2,1)S(1)}, u32[]{:S(2)}, u32[]{:S(2)}) collective-permute-start(bf16[1,256,2048]{2,1,0:T(8,128)(2,1)S(1)} %slice_bitcast_fusion), channel_id=1, source_target_pairs={{0,16},{1,17},{2,18},{3,19},{4,20},{5,21},{6,22},{7,23},{8,24},{9,... | collective-permute-start | bytes 3145736 | tf_op jit(solution)/shard_map/ppermute | solution.py:14
  120.7 26.0 %collective-permute-start.1 = (bf16[1,256,2048]{2,1,0:T(8,128)(2,1)S(1)}, bf16[1,256,2048]{2,1,0:T(8,128)(2,1)S(1)}, u32[]{:S(2)}, u32[]{:S(2)}) collective-permute-start(bf16[1,256,2048]{2,1,0:T(8,128)(2,1)S(1)} %slice_bitcast_fusion), channel_id=1, source_target_pairs={{16,0},{17,1},{18,2},{19,3},{20,4},{21,5},{22,6},{23,7},{24,8},{25... | collective-permute-start | bytes 3145736 | tf_op jit(solution)/shard_map/ppermute | solution.py:17
  124.9 36.8 %collective-permute-start.2 = (bf16[1,256,2048]{2,1,0:T(8,128)(2,1)S(1)}, bf16[1,256,2048]{2,1,0:T(8,128)(2,1)S(1)}, u32[]{:S(2)}, u32[]{:S(2)}) collective-permute-start(bf16[1,256,2048]{2,1,0:T(8,128)(2,1)S(1)} %slice_bitcast_fusion), channel_id=1, source_target_pairs={{0,1},{1,2},{2,3},{3,4},{4,5},{5,6},{6,7},{7,8},{8,9},{9,10},{10,1... | collective-permute-start | bytes 3145736 | tf_op jit(solution)/shard_map/ppermute | solution.py:14
  127.8 37.8 %collective-permute-start.3 = (bf16[1,256,2048]{2,1,0:T(8,128)(2,1)S(1)}, bf16[1,256,2048]{2,1,0:T(8,128)(2,1)S(1)}, u32[]{:S(2)}, u32[]{:S(2)}) collective-permute-start(bf16[1,256,2048]{2,1,0:T(8,128)(2,1)S(1)} %slice_bitcast_fusion), channel_id=1, source_target_pairs={{1,0},{2,1},{3,2},{4,3},{5,4},{6,5},{7,6},{8,7},{9,8},{10,9},{11,1... | collective-permute-start | bytes 3145736 | tf_op jit(solution)/shard_map/ppermute | solution.py:17
Sparse Core Ops, SparseCore 0:
  9.6 101.3 all-gather.2
  113.2 59.5 all-gather.4
where the time goes:
time: 196 us
  waiting for transfers between devices  135 us (69%)
  matrix products  29 us (15%)
  between operations  14.1 us (7%)
  starting transfers between devices  10.4 us (5%)
  other arithmetic  6.84 us (3%)
    all_gather x1, waiting for transfers between devices, per_device(): lax.all_gather(w_qkv, 'inner', axis=0, tiled=True)  101 us
    ppermute x2, waiting for transfers between devices, padded(): lax.ppermute(lax.slice_in_dim(block, block.shape[dim] - width, None, axis...  29.2 us
    dot_general x40, matrix products, per_device(): jnp.dot(rounded[:, slot_no * rows_here:(slot_no + 1) * rows_here], candid...  9.07 us
    dot_general x1, matrix products, per_device(): jnp.dot(normed, lax.all_gather(w_qkv, 'inner', axis=0, tiled=True), prefe...  8.16 us
    dot_general x40, matrix products, per_device(): jnp.einsum('qd,kd->qk', query_head, source_kv[:, offset_q:offset_q + head...  7.37 us
    ppermute x2, starting transfers between devices, padded(): lax.ppermute(lax.slice_in_dim(block, 0, width, axis=dim), axis, backward)  6.22 us
    dot_general x1, matrix products, per_device(): jnp.dot(context_all, lax.all_gather(w_out, 'inner', axis=1, tiled=True),...  4.41 us
    reduce_sum x2, other arithmetic, per_device(): totals = jnp.sum(weights, axis=1, keepdims=True)  4.26 us
  transfers between devices with their start and end apart: 6, of which 5 were waited for; matrix products, arithmetic and copies ran while one was open for 16% of the time, Pallas kernels for 0%

commit v1 on v0

v1 whole, which is shorter than its diff:
```python
import functools

import jax
import jax.numpy as jnp
from jax import lax
from jax.experimental import pallas as pl
from jax.experimental.pallas import tpu as pltpu
from jax.sharding import PartitionSpec as P

HD = 128
PAIR = 2 * HD
VMEM = pl.BlockSpec(memory_space=pltpu.VMEM)
SMEM = pl.BlockSpec(memory_space=pltpu.SMEM)
HBM = pl.BlockSpec(memory_space=pltpu.HBM)
MARK = 16
BF16 = jnp.bfloat16
F32 = jnp.float32


def place():
    inner = lax.axis_index("inner")
    side = lax.rem(lax.axis_index("outer"), 2)
    return side, lax.rem(lax.div(inner, 2), 2), lax.rem(inner, 2)


def ring_source(step, count):
    z = lax.div(lax.axis_index("inner"), 4)
    at = jnp.where(lax.rem(z, 2) == 0, lax.div(z, 2), count - 1 - lax.div(z, 2))
    at = lax.rem(at - step + count, count)
    return jnp.where(2 * at < count, 2 * at, 2 * (count - at) - 1)


def along_ring(x):
    count = lax.axis_size("inner") // 4
    order = [z for z in range(0, count, 2)] + [z for z in range(count - 1, 0, -1) if z % 2]
    pairs = [
        (4 * z + j, 4 * order[(n + 1) % count] + j) for n, z in enumerate(order) for j in range(4)
    ]
    return lax.ppermute(x, "inner", pairs)


def swap(x, r):
    inner = lax.axis_size("inner")
    if r < 4:
        return lax.ppermute(x, "inner", [(i, i ^ r) for i in range(inner)])
    pairs = [
        (o * inner + i, (o ^ 1) * inner + (i ^ (r & 3)))
        for o in range(lax.axis_size("outer"))
        for i in range(inner)
    ]
    return lax.ppermute(x, ("outer", "inner"), pairs)


def swap_by_core(x, r_0, r_1):
    inner = lax.axis_size("inner")
    pairs = []
    for o in range(lax.axis_size("outer")):
        for i in range(inner):
            r = r_1 if i % 2 else r_0
            pairs.append((o * inner + i, (o ^ (r >> 2)) * inner + (i ^ (r & 3))))
    return lax.ppermute(x, ("outer", "inner"), pairs)


def to_next_group(x):
    inner = lax.axis_size("inner")
    pairs = [(i, i + 3 if i % 2 else i - 3) for i in range(inner)]
    return lax.ppermute(x, "inner", [p for p in pairs if 0 <= p[1] < inner])


def along_outer(x, shift):
    outer = lax.axis_size("outer")
    pairs = [(o, o + shift) for o in range(outer) if 0 <= o + shift < outer]
    return lax.ppermute(x, "outer", pairs)


def after(x, *others):
    return lax.optimization_barrier((x,) + others)[0]


def call(body, shapes, args, specs=None, scratch=(), limit=16, cost=0.0):
    many = isinstance(shapes, list)
    outs = [jax.ShapeDtypeStruct(s, BF16) for s in (shapes if many else [shapes])]
    return pl.pallas_call(
        body,
        out_shape=outs if many else outs[0],
        in_specs=specs or [VMEM] * len(args),
        out_specs=[VMEM] * len(outs) if many else VMEM,
        scratch_shapes=list(scratch),
        compiler_params=pltpu.CompilerParams(vmem_limit_bytes=limit * 1024 * 1024),
        cost_estimate=pl.CostEstimate(
            flops=1000, bytes_accessed=int(3.5e6 * cost) + 1000, transcendentals=0
        ),
    )(*args)


def norm_body(x, listed, out):
    marks = jnp.concatenate(
        [listed[...].astype(F32), jnp.zeros((1, HD - listed.shape[1]), F32)], axis=1
    )
    out[:MARK, :] = jnp.zeros((MARK, out.shape[1]), BF16)
    out[:MARK, :HD] = jnp.broadcast_to(marks, (MARK, HD)).astype(BF16)
    values = x[...].astype(F32)
    center = values - jnp.mean(values, axis=-1, keepdims=True)
    spread = jnp.mean(center * center, axis=-1, keepdims=True)
    out[MARK:, :] = (center * lax.rsqrt(spread + 1e-05)).astype(BF16)


def pick_body(w, mine, send, sems):
    side, y, _ = place()
    wide = w.shape[1] // 3
    copies = []
    for out, which in ((send, 1 - y), (mine, y)):
        for part in range(3):
            column = pl.multiple_of(part * wide + (4 * side + 2 * which) * HD, HD)
            into = out.at[:, pl.ds(part * PAIR, PAIR)]
            copies.append(pltpu.make_async_copy(w.at[:, pl.ds(column, PAIR)], into, sems.at[len(copies)]))
    for copy in copies:
        copy.start()
    for copy in copies:
        copy.wait()


def stack_body(*refs):
    for n, ref in enumerate(refs[:-1]):
        refs[-1][n] = ref[...]


def stack(arrays):
    return call(stack_body, (len(arrays),) + arrays[0].shape, arrays, limit=8)


def gather_weight(pieces, weight, count):
    _, y, core = place()
    rows = pieces[0].shape[0] // 2
    for n, piece in enumerate(pieces):
        which_core = 1 - core if n // count else core
        for half, which_y in ((0, y), (1, 1 - y)):
            into = 4 * ring_source(n % count, count) + 2 * which_y + which_core
            into = pl.ds(pl.multiple_of(into * rows, 16), rows)
            weight[into, :] = piece[half * rows : (half + 1) * rows, :]


def project_body(count, *refs):
    pieces, blocks = refs[: 2 * count], refs[2 * count : 2 * count + 4]
    q, marks, *kv, halo, halo_across, weight = refs[2 * count + 4 :]
    gather_weight(pieces, weight, count)
    for n, block in enumerate(blocks):
        done = jnp.dot(block[MARK:, :], weight[...], preferred_element_type=F32).astype(BF16)
        q[n] = done[:, :PAIR]
        kv[n][...] = done[:, PAIR:]
        marks[n] = block[:MARK, :HD]
    _, y, core = place()
    halo[...] = jnp.where(y == core, kv[0][...], kv[1][...])
    halo_across[...] = jnp.where(y == core, kv[2][...], kv[3][...])


def attend(q, keys_values):
    scores = []
    for key, _, length in keys_values:
        score = lax.dot_general(q, key, (((1,), (1,)), ((), ())), preferred_element_type=F32)
        position = lax.broadcasted_iota(jnp.int32, (1, score.shape[1]), 1)
        scores.append(jnp.where(position < length, score, -jnp.inf))
    largest = functools.reduce(jnp.maximum, scores)
    largest = jnp.max(largest, axis=1, keepdims=True)
    factor = float(HD) ** -0.5 * 1.4426950408889634
    total, context = 0.0, 0.0
    for score, (_, value, _) in zip(scores, keys_values):
        weight = jnp.exp2((score - largest) * factor)
        total = total + jnp.sum(weight, axis=1, keepdims=True)
        context = context + jnp.dot(weight.astype(BF16), value, preferred_element_type=F32)
    return (context / total).astype(BF16)


def attend_body(blocks, wider, counts, *refs):
    q, marks, kv, other, halo = *refs[:2], refs[2:6], refs[6:10], refs[10:12]
    beyond, outs, far = refs[12:16], refs[-1 - len(blocks) : -1], refs[-1]
    side, y, core = place()
    inner = lax.axis_size("inner")
    for b, out in zip(blocks, outs):
        which_side, which_y = lax.rem(side + b // 2, 2), lax.rem(y + b % 2, 2)
        number = (lax.axis_index("outer") - side + which_side) * inner
        number = number + lax.axis_index("inner") - 2 * y + 2 * which_y
        far[...] = jnp.where(which_y == core, halo[b // 2][...], other[b ^ 1][...])
        mark = marks[b, 0:1, :].astype(F32)
        slots = [mark[:, n : n + 1] for n in range(5)]
        sources = [
            (kv[b], slots[0], number),
            (kv[b ^ 2], jnp.where(which_side == 0, slots[2], slots[1]), number + inner * (1 - 2 * which_side)),
            (other[b], jnp.where(core == 0, slots[4], slots[3]), number + 1 - 2 * core),
            (far, jnp.where(core == 0, slots[3], slots[4]), number - 1 + 2 * core),
        ]
        if wider:
            far_outer = jnp.where(which_side == 0, beyond[b % 2][...], beyond[2 + b % 2][...])
            mark_outer = jnp.where(which_side == 0, slots[1], slots[2])
            sources.append((far_outer, mark_outer, number - inner * (1 - 2 * which_side)))
        for head in range(2):
            at = head * HD
            keys_values = []
            for source, listed, at_block in sources:
                count = counts[jnp.clip(at_block, 0, counts.shape[0] - 1)]
                length = jnp.where(jnp.broadcast_to(listed, (1, source.shape[0])) >= 0, count, 0)
                keys_values.append(
                    (source[:, at : at + HD], source[:, PAIR + at : PAIR + at + HD], length)
                )
            out[:, at : at + HD] = attend(q[b, :, at : at + HD], keys_values)


def finish_body(count, *refs):
    contexts, refs = refs[:4], refs[4:]
    out, context = refs[-2:]
    bundles = refs[:-2]
    side, y, core = place()
    for b, piece in enumerate(contexts):
        pair = 2 * lax.rem(side + b // 2, 2) + lax.rem(y + b % 2, 2)
        context[pair] = piece[...]
    whole = jnp.concatenate([context[pair] for pair in range(4)], axis=1)
    here, here_next, *there = bundles
    for step in range(count):
        z = ring_source(step, count)
        pair = (there[0][...], there[1][...]) if step == 0 else (there[2][step - 1], there[3][step - 1])
        for which_y, mine, other in ((y, here[step], here_next[step]), (1 - y, *pair)):
            tile = jnp.concatenate(
                [jnp.where(core == 0, mine, other), jnp.where(core == 0, other, mine)], axis=1
            )
            column = pl.multiple_of((4 * z + 2 * which_y) * HD, HD)
            done = jnp.dot(whole, tile, preferred_element_type=F32)
            out[:, pl.ds(column, PAIR)] = done.astype(BF16)


def per_device(tokens, w_qkv, w_out, neighbours, counts):
    rows, width = tokens.shape
    heads_all = w_out.shape[0]
    wide = 3 * PAIR
    count = lax.axis_size("inner") // 4
    wider = lax.axis_size("outer") > 2
    w_rows = w_qkv.shape[0]
    side, _, core = place()

    normed = call(norm_body, (MARK + rows, width), [tokens, neighbours], limit=8)
    mine, send = call(
        pick_body,
        [(w_rows, wide)] * 2,
        [after(w_qkv, normed)],
        specs=[pl.BlockSpec(memory_space=pl.ANY)],
        scratch=[pltpu.SemaphoreType.DMA((6,))],
        limit=8,
    )
    block_x = swap(normed, 4)
    got = swap(send, 2)
    strips = [w_out]
    if count > 1:
        strips.append(along_ring(after(w_out, normed)))
    block_y = swap(after(normed, got, *strips[1:]), 2)
    pieces = [stack([mine, after(got, *strips[1:])]).reshape(2 * w_rows, wide)]
    for _ in range(count - 1):
        pieces.append(along_ring(pieces[-1]))
    next_pieces = [swap(p, 1) for p in pieces]
    block_d = jnp.where(core == 0, block_y, block_x)
    for n in range(1, count - 2):
        strips.append(along_ring(strips[-1]))
    block_d = after(block_d, *strips[1:], *pieces[: count - 1], *next_pieces[: count - 2])
    block_d = swap_by_core(block_d, 4, 2)
    for n in range(len(strips), count):
        strips.append(along_ring(after(strips[-1], pieces[-1])))
    there = [swap(after(w_out, pieces[-1]), 2)]
    pieces = pieces + next_pieces

    q, marks, *kv, halo, halo_across = call(
        functools.partial(project_body, count),
        [(4, rows, PAIR), (4, MARK, HD)] + [(rows, 2 * PAIR)] * 6,
        pieces + [normed, block_y, block_x, block_d],
        scratch=[pltpu.VMEM((width, wide), BF16)],
        cost=5.0,
    )
    here = stack([after(strips[0], halo)] + strips[1:])
    here_next = swap(here, 1)
    if count > 1:
        there.append(swap(after(stack([after(strips[1], halo)] + strips[2:]), there[0]), 2))
    halo, halo_across = to_next_group(halo), to_next_group(halo_across)
    next_kv = [swap(b, 1) for b in kv]
    beyond = []
    if wider:
        upper = [jnp.where(side == 1, kv[b], kv[b + 2]) for b in range(2)]
        lower = [jnp.where(side == 0, kv[b], kv[b + 2]) for b in range(2)]
        beyond = [along_outer(b, 2) for b in upper] + [along_outer(b, -2) for b in lower]

    def attended(blocks, halo, halo_across):
        held = [counts, q, marks] + kv + next_kv + [halo, halo_across] + beyond
        return call(
            functools.partial(attend_body, blocks, wider),
            [(rows, PAIR)] * len(blocks),
            held,
            specs=[SMEM] + [VMEM] * (len(held) - 1),
            scratch=[pltpu.VMEM((rows, 2 * PAIR), BF16)],
            cost=2.5,
        )

    c_1, c_0 = attended((1, 0), halo, halo)
    c_3, c_2 = attended((3, 2), after(halo, c_1), halo_across)
    contexts = [c_0, swap(c_1, 2), swap(c_2, 4), swap(c_3, 6)]
    there_next = swap(after(there[1], *contexts[1:]), 1) if count > 1 else None
    bundles = [here, here_next, there[0], swap(there[0], 1)]
    bundles += [there[1], there_next] if count > 1 else []
    return call(
        functools.partial(finish_body, count),
        (rows, width),
        contexts + bundles,
        scratch=[pltpu.VMEM((4, rows, PAIR), BF16)],
        cost=1.0,
    )


def solution(mesh):
    placed = (
        P(("outer", "inner"), None),
        P("inner", None),
        P(None, "inner"),
        P(("outer", "inner"), None),
        P(),
    )
    return jax.shard_map(
        per_device,
        mesh=mesh,
        in_specs=placed,
        out_specs=P(("outer", "inner"), None),
        check_vma=False,
    )
```

time: 196 us -> 93 us (0.47)
  the two profiles are of different devices: /device:TPU:19 before, /device:TPU:0 now
where the time goes in v1:
time: 93 us; the launch traced here: 92.7 us
  waiting for transfers between devices  37.6 us (40%)
  starting transfers between devices  36.7 us (39%)
  Pallas kernels  15.9 us (17%)
  local copies, waits for them, and re-layouts  2.22 us (2%)
    ppermute x6, starting transfers between devices, along_ring(): return lax.ppermute(x, 'inner', pairs)  17.2 us
    pallas_call x9, Pallas kernels, call(): pl.pallas_call(body, out_shape=outs if many else outs[0], in_specs=specs...  15.9 us
    ppermute x6, waiting for transfers between devices, along_ring(): return lax.ppermute(x, 'inner', pairs)  15.5 us
    ppermute x16, waiting for transfers between devices, swap(): return lax.ppermute(x, 'inner', [(i, i ^ r) for i in range(inner)])  13.2 us
    ppermute x16, starting transfers between devices, swap(): return lax.ppermute(x, 'inner', [(i, i ^ r) for i in range(inner)])  12.8 us
    ppermute x3, waiting for transfers between devices, swap(): return lax.ppermute(x, ('outer', 'inner'), pairs)  8.16 us
    ppermute x3, starting transfers between devices, swap(): return lax.ppermute(x, ('outer', 'inner'), pairs)  3.79 us
    unnamed x12, local copies, waits for them, and re-layouts  2.22 us
  transfers between devices with their start and end apart: 28, of which 13 were waited for; matrix products, arithmetic and copies ran while one was open for 0% of the time, Pallas kernels for 14%

profile of v1, /device:TPU:0, one launch (start us, length us, event | category | flops | bytes accessed | tf_op | source)
XLA Modules:
  0.0 92.7 jit_solution(17085302465385257554)
XLA Ops:
  0.0 1.2 %copy-done = bf16[256,2048]{1,0:T(8,128)(2,1)S(1)} copy-done((bf16[256,2048]{1,0:T(8,128)(2,1)S(1)}, bf16[256,2048]{1,0:T(8,128)(2,1)}, u32[]{:S(2)}) %copy-start) | copy-done | bytes 1048600
  1.2 0.7 copy-done.5
  1.9 0.6 shard_map.55.refs_8_
  2.5 0.3 copy-done.2
  2.8 4.0 %collective-permute-start.1 = (bf16[1024,128]{1,0:T(8,128)(2,1)S(1)}, bf16[1024,128]{1,0:T(8,128)(2,1)}, u32[]{:S(2)}, u32[]{:S(2)}) collective-permute-start(bf16[1024,128]{1,0:T(8,128)(2,1)S(1)} %copy-done.2), channel_id=1, source_target_pairs={{0,8},{1,9},{2,10},{3,11},{8,12},{9,13},{10,14},{11,15},{12,4},{13... | collective-permute-start | bytes 786440 | tf_op jit(solution)/shard_map/ppermute | solution.py:39
  6.9 0.1 shard_map.56
  7.0 1.6 %collective-permute-start = (bf16[128,768]{1,0:T(8,128)(2,1)S(1)}, bf16[128,768]{1,0:T(8,128)(2,1)S(1)}, u32[]{:S(2)}, u32[]{:S(2)}) collective-permute-start(bf16[128,768]{1,0:T(8,128)(2,1)S(1)} %get-tuple-element.33), channel_id=1, source_target_pairs={{0,2},{1,3},{2,0},{3,1},{4,6},{5,7},{6,4},{7,5},{8,10},{9,11},{10,... | collective-permute-start | bytes 589832 | tf_op jit(solution)/shard_map/ppermute | solution.py:45
  8.6 1.5 %collective-permute-start.10 = (bf16[272,2048]{1,0:T(8,128)(2,1)S(1)}, bf16[272,2048]{1,0:T(8,128)(2,1)S(1)}, u32[]{:S(2)}, u32[]{:S(2)}) collective-permute-start(bf16[272,2048]{1,0:T(8,128)(2,1)S(1)} %shard_map.55.refs_8_), channel_id=1, source_target_pairs={{0,16},{1,17},{2,18},{3,19},{4,20},{5,21},{6,22},{7,23},{8,24},{9,... | collective-permute-start | bytes 3342344 | tf_op jit(solution)/shard_map/ppermute | solution.py:51
  10.1 3.4 %collective-permute-done.refs_1_ = bf16[128,768]{1,0:T(8,128)(2,1)S(1)} collective-permute-done((bf16[128,768]{1,0:T(8,128)(2,1)S(1)}, bf16[128,768]{1,0:T(8,128)(2,1)S(1)}, u32[]{:S(2)}, u32[]{:S(2)}) %collective-permute-start) | collective-permute-done | bytes 196640 | tf_op jit(solution)/shard_map/ppermute | solution.py:45
  13.4 1.5 %collective-permute-start.9 = (bf16[272,2048]{1,0:T(8,128)(2,1)S(1)}, bf16[272,2048]{1,0:T(8,128)(2,1)S(1)}, u32[]{:S(2)}, u32[]{:S(2)}) collective-permute-start(bf16[272,2048]{1,0:T(8,128)(2,1)S(1)} %shard_map.55.refs_8_), channel_id=1, source_target_pairs={{0,2},{1,3},{2,0},{3,1},{4,6},{5,7},{6,4},{7,5},{8,10},{9,11},{10,... | collective-permute-start | bytes 3342344 | tf_op jit(solution)/shard_map/ppermute | solution.py:45
  15.0 0.8 shard_map.57
  15.7 2.5 %collective-permute-start.2 = (bf16[256,768]{1,0:T(8,128)(2,1)}, bf16[256,768]{1,0:T(8,128)(2,1)}, u32[]{:S(2)}, u32[]{:S(2)}) collective-permute-start(bf16[256,768]{1,0:T(8,128)(2,1)} %bitcast.refs_0_), channel_id=1, source_target_pairs={{0,8},{1,9},{2,10},{3,11},{8,12},{9,13},{10,14},{11,15},{12,4},{13... | collective-permute-start | bytes 1179656 | tf_op jit(solution)/shard_map/ppermute | solution.py:39
  18.2 0.7 collective-permute-start.11
  18.9 9.2 %collective-permute-done.2.refs_1_ = bf16[256,768]{1,0:T(8,128)(2,1)} collective-permute-done((bf16[256,768]{1,0:T(8,128)(2,1)}, bf16[256,768]{1,0:T(8,128)(2,1)}, u32[]{:S(2)}, u32[]{:S(2)}) %collective-permute-start.2) | collective-permute-done | bytes 393248 | tf_op jit(solution)/shard_map/ppermute | solution.py:39
  28.1 3.4 %collective-permute-start.3 = (bf16[256,768]{1,0:T(8,128)(2,1)}, bf16[256,768]{1,0:T(8,128)(2,1)S(1)}, u32[]{:S(2)}, u32[]{:S(2)}) collective-permute-start(bf16[256,768]{1,0:T(8,128)(2,1)} %collective-permute-done.2.refs_1_), channel_id=1, source_target_pairs={{0,8},{1,9},{2,10},{3,11},{8,12},{9,13},{10,14},{11,15},{12,4},{13... | collective-permute-start | bytes 1179656 | tf_op jit(solution)/shard_map/ppermute | solution.py:39
  31.5 2.9 %collective-permute-done.10.refs_10_ = bf16[272,2048]{1,0:T(8,128)(2,1)S(1)} collective-permute-done((bf16[272,2048]{1,0:T(8,128)(2,1)S(1)}, bf16[272,2048]{1,0:T(8,128)(2,1)S(1)}, u32[]{:S(2)}, u32[]{:S(2)}) %collective-permute-start.10) | collective-permute-done | bytes 1114144 | tf_op jit(solution)/shard_map/ppermute | solution.py:51
  34.3 4.3 %collective-permute-done.9.refs_9_ = bf16[272,2048]{1,0:T(8,128)(2,1)S(1)} collective-permute-done((bf16[272,2048]{1,0:T(8,128)(2,1)S(1)}, bf16[272,2048]{1,0:T(8,128)(2,1)S(1)}, u32[]{:S(2)}, u32[]{:S(2)}) %collective-permute-start.9) | collective-permute-done | bytes 1114144 | tf_op jit(solution)/shard_map/ppermute | solution.py:45
  38.7 0.1 broadcast_select_fusion
  38.8 1.0 %collective-permute-done.3.refs_2_ = bf16[256,768]{1,0:T(8,128)(2,1)S(1)} collective-permute-done((bf16[256,768]{1,0:T(8,128)(2,1)}, bf16[256,768]{1,0:T(8,128)(2,1)S(1)}, u32[]{:S(2)}, u32[]{:S(2)}) %collective-permute-start.3) | collective-permute-done | bytes 393248 | tf_op jit(solution)/shard_map/ppermute | solution.py:39
  39.8 1.5 %collective-permute-start.12 = (bf16[272,2048]{1,0:T(8,128)(2,1)S(1)}, bf16[272,2048]{1,0:T(8,128)(2,1)S(1)}, u32[]{:S(2)}, u32[]{:S(2)}) collective-permute-start(bf16[272,2048]{1,0:T(8,128)(2,1)S(1)} %broadcast_select_fusion), channel_id=1, source_target_pairs={{0,16},{1,3},{2,18},{3,1},{4,20},{5,7},{6,22},{7,5},{8,24},{9,11},... | collective-permute-start | bytes 3342344 | tf_op jit(solution)/shard_map/ppermute | solution.py:61
  41.3 3.3 %collective-permute-start.4 = (bf16[256,768]{1,0:T(8,128)(2,1)S(1)}, bf16[256,768]{1,0:T(8,128)(2,1)S(1)}, u32[]{:S(2)}, u32[]{:S(2)}) collective-permute-start(bf16[256,768]{1,0:T(8,128)(2,1)S(1)} %collective-permute-done.3.refs_2_), channel_id=1, source_target_pairs={{0,8},{1,9},{2,10},{3,11},{8,12},{9,13},{10,14},{11,15},{12,4},{13... | collective-permute-start | bytes 1179656 | tf_op jit(solution)/shard_map/ppermute | solution.py:39
  44.6 5.3 %collective-permute-done.4.refs_3_ = bf16[256,768]{1,0:T(8,128)(2,1)S(1)} collective-permute-done((bf16[256,768]{1,0:T(8,128)(2,1)S(1)}, bf16[256,768]{1,0:T(8,128)(2,1)S(1)}, u32[]{:S(2)}, u32[]{:S(2)}) %collective-permute-start.4) | collective-permute-done | bytes 393248 | tf_op jit(solution)/shard_map/ppermute | solution.py:39
  49.9 3.4 %collective-permute-start.22 = (bf16[1024,128]{1,0:T(8,128)(2,1)S(1)}, bf16[1024,128]{1,0:T(8,128)(2,1)S(1)}, u32[]{:S(2)}, u32[]{:S(2)}) collective-permute-start(bf16[1024,128]{1,0:T(8,128)(2,1)S(1)} %collective-permute-done.11.refs_2_.refs_1_), channel_id=1, source_target_pairs={{0,8},{1,9},{2,10},{3,11},{8,12},{9,13},{10,14},{11,15},{12,4},{13... | collective-permute-start | bytes 786440 | tf_op jit(solution)/shard_map/ppermute | solution.py:39
  53.2 1.3 %collective-permute-start.24 = (bf16[1024,128]{1,0:T(8,128)(2,1)S(1)}, bf16[1024,128]{1,0:T(8,128)(2,1)S(1)}, u32[]{:S(2)}, u32[]{:S(2)}) collective-permute-start(bf16[1024,128]{1,0:T(8,128)(2,1)S(1)} %copy-done.3), channel_id=1, source_target_pairs={{0,2},{1,3},{2,0},{3,1},{4,6},{5,7},{6,4},{7,5},{8,10},{9,11},{10,... | collective-permute-start | bytes 786440 | tf_op jit(solution)/shard_map/ppermute | solution.py:45
  54.5 0.8 collective-permute-done.12.refs_11_
  55.3 4.8 %shard_map.58 = (bf16[4,256,256]{2,1,0:T(8,128)(2,1)S(1)}, bf16[4,16,128]{2,1,0:T(8,128)(2,1)S(1)}, bf16[256,512]{1,0:T(8,128)(2,1)S(1)}, bf16[256,512]{1,0:T(8,...) custom-call(bf16[256,768]{1,0:T(8,128)(2,1)} %bitcast.refs_0_, ...), custom_call_target="tpu_custom_call" | custom-call | flops 1000 | bytes 17501000 | tf_op jit(solution)/shard_map/pallas_call | solution.py:83
  60.1 1.0 %shard_map.62 = bf16[3,1024,128]{2,1,0:T(8,128)(2,1)S(1)} custom-call(bf16[1024,128]{1,0:T(8,128)(2,1)} %collective-permute-done.1.refs_1_.refs_0_, bf16[1024,128]{1,0:T(8,128)(2,1)S(1)} %collective-permute-done.11.refs_2_.refs_1_, bf16[1024,128]{1,0:T(8,128)(2,1)S(1)} %collective-permute-done.22.refs_3_.refs_2_), custom_call_target="tpu_custom_call" | custom-call | flops 1000 | bytes 1000 | tf_op jit(solution)/shard_map/pallas_call | solution.py:83
  61.1 0.6 collective-permute-done.24.refs_6_
  61.7 1.3 %collective-permute-start.26 = (bf16[3,1024,128]{2,1,0:T(8,128)(2,1)S(1)}, bf16[3,1024,128]{2,1,0:T(8,128)(2,1)S(1)}, u32[]{:S(2)}, u32[]{:S(2)}) collective-permute-start(bf16[3,1024,128]{2,1,0:T(8,128)(2,1)S(1)} %shard_map.62), channel_id=1, source_target_pairs={{0,2},{1,3},{2,0},{3,1},{4,6},{5,7},{6,4},{7,5},{8,10},{9,11},{10,... | collective-permute-start | bytes 2359304 | tf_op jit(solution)/shard_map/ppermute | solution.py:45
  62.9 0.5 collective-permute-start.14
  63.5 0.5 collective-permute-start.16
  64.0 0.5 collective-permute-done.13.refs_6_
  64.5 0.7 collective-permute-start.17
  65.2 0.7 collective-permute-start.19
  65.9 1.0 %shard_map.61.refs_4_ = bf16[4,1024,128]{2,1,0:T(8,128)(2,1)S(1)} custom-call(bf16[1024,128]{1,0:T(8,128)(2,1)S(1)} %copy-done.3, bf16[1024,128]{1,0:T(8,128)(2,1)} %collective-permute-done.1.refs_1_.refs_0_, bf16[1024,128]{1,0:T(8,128)(2,1)S(1)} %collective-permute-done.11.refs_2_.refs_1_, bf16[1024,128]{1,0:T(8,128)(2,1)S(1)} %collective-permute-done.22.refs_3_.refs_2_), custom_call_target="tpu_custom_call" | custom-call | flops 1000 | bytes 1000 | tf_op jit(solution)/shard_map/pallas_call | solution.py:83
  66.9 4.4 %collective-permute-start.23 = (bf16[4,1024,128]{2,1,0:T(8,128)(2,1)S(1)}, bf16[4,1024,128]{2,1,0:T(8,128)(2,1)S(1)}, u32[]{:S(2)}, u32[]{:S(2)}) collective-permute-start(bf16[4,1024,128]{2,1,0:T(8,128)(2,1)S(1)} %shard_map.61.refs_4_), channel_id=1, source_target_pairs={{0,1},{1,0},{2,3},{3,2},{4,5},{5,4},{6,7},{7,6},{8,9},{9,8},{10,11... | collective-permute-start | bytes 3145736 | tf_op jit(solution)/shard_map/ppermute | solution.py:45
  71.3 2.6 %shard_map.59 = (bf16[256,256]{1,0:T(8,128)(2,1)S(1)}, bf16[256,256]{1,0:T(8,128)(2,1)S(1)}) custom-call(s32[32]{0:T(128)S(1)} %copy-done.4, bf16[4,256,256]{2,1,0:T(8,128)(2,1)S(1)} %get-tuple-element.38.refs_0_, bf16[4,16,128]{2,1,0:T(8,128)(2,1)S(1)} %get-tuple-element.39.refs_1_, bf16[256,512]{1,0:T(8,128)(2,1)S(1)} %get-tuple-element.40.refs_2_, ...), custom_call_target="tpu_custom_call" | custom-call | flops 1000 | bytes 8751000 | tf_op jit(solution)/shard_map/pallas_call | solution.py:83
  73.9 2.6 %shard_map.60 = (bf16[256,256]{1,0:T(8,128)(2,1)S(1)}, bf16[256,256]{1,0:T(8,128)(2,1)S(1)}) custom-call(s32[32]{0:T(128)S(1)} %copy-done.4, bf16[4,256,256]{2,1,0:T(8,128)(2,1)S(1)} %get-tuple-element.38.refs_0_, bf16[4,16,128]{2,1,0:T(8,128)(2,1)S(1)} %get-tuple-element.39.refs_1_, bf16[256,512]{1,0:T(8,128)(2,1)S(1)} %get-tuple-element.40.refs_2_, ...), custom_call_target="tpu_custom_call" | custom-call | flops 1000 | bytes 8751000 | tf_op jit(solution)/shard_map/pallas_call | solution.py:83
  76.6 1.6 %collective-permute-start.20 = (bf16[256,256]{1,0:T(8,128)(2,1)S(1)}, bf16[256,256]{1,0:T(8,128)(2,1)S(1)}, u32[]{:S(2)}, u32[]{:S(2)}) collective-permute-start(bf16[256,256]{1,0:T(8,128)(2,1)S(1)} %get-tuple-element.49), channel_id=1, source_target_pairs={{0,16},{1,17},{2,18},{3,19},{4,20},{5,21},{6,22},{7,23},{8,24},{9,... | collective-permute-start | bytes 393224 | tf_op jit(solution)/shard_map/ppermute | solution.py:51
  78.1 0.7 collective-permute-start.21
  78.9 1.3 %collective-permute-start.18 = (bf16[256,256]{1,0:T(8,128)(2,1)S(1)}, bf16[256,256]{1,0:T(8,128)(2,1)S(1)}, u32[]{:S(2)}, u32[]{:S(2)}) collective-permute-start(bf16[256,256]{1,0:T(8,128)(2,1)S(1)} %get-tuple-element.46), channel_id=1, source_target_pairs={{0,2},{1,3},{2,0},{3,1},{4,6},{5,7},{6,4},{7,5},{8,10},{9,11},{10,... | collective-permute-start | bytes 393224 | tf_op jit(solution)/shard_map/ppermute | solution.py:45
  80.1 2.1 %collective-permute-done.20.refs_2_ = bf16[256,256]{1,0:T(8,128)(2,1)S(1)} collective-permute-done((bf16[256,256]{1,0:T(8,128)(2,1)S(1)}, bf16[256,256]{1,0:T(8,128)(2,1)S(1)}, u32[]{:S(2)}, u32[]{:S(2)}) %collective-permute-start.20) | collective-permute-done | bytes 131104 | tf_op jit(solution)/shard_map/ppermute | solution.py:51
  82.2 3.2 %collective-permute-done.21.refs_3_ = bf16[256,256]{1,0:T(8,128)(2,1)S(1)} collective-permute-done((bf16[256,256]{1,0:T(8,128)(2,1)S(1)}, bf16[256,256]{1,0:T(8,128)(2,1)S(1)}, u32[]{:S(2)}, u32[]{:S(2)}) %collective-permute-start.21) | collective-permute-done | bytes 131104 | tf_op jit(solution)/shard_map/ppermute | solution.py:51
  85.4 2.2 %collective-permute-done.18.refs_1_ = bf16[256,256]{1,0:T(8,128)(2,1)S(1)} collective-permute-done((bf16[256,256]{1,0:T(8,128)(2,1)S(1)}, bf16[256,256]{1,0:T(8,128)(2,1)S(1)}, u32[]{:S(2)}, u32[]{:S(2)}) %collective-permute-start.18) | collective-permute-done | bytes 131104 | tf_op jit(solution)/shard_map/ppermute | solution.py:45
  87.6 0.2 collective-permute-start.27
  87.9 0.3 collective-permute-start.25
  88.1 2.1 %collective-permute-done.25.refs_7_ = bf16[1024,128]{1,0:T(8,128)(2,1)S(1)} collective-permute-done((bf16[1024,128]{1,0:T(8,128)(2,1)S(1)}, bf16[1024,128]{1,0:T(8,128)(2,1)S(1)}, u32[]{:S(2)}, u32[]{:S(2)}) %collective-permute-start.25) | collective-permute-done | bytes 262176 | tf_op jit(solution)/shard_map/ppermute | solution.py:45
  90.3 2.4 %shard_map.63 = bf16[256,2048]{1,0:T(8,128)(2,1)} custom-call(bf16[256,256]{1,0:T(8,128)(2,1)S(1)} %get-tuple-element.45.refs_0_, bf16[256,256]{1,0:T(8,128)(2,1)S(1)} %collective-permute-done.18.refs_1_, bf16[256,256]{1,0:T(8,128)(2,1)S(1)} %collective-permute-done.20.refs_2_, bf16[256,256]{1,0:T(8,128)(2,1)S(1)} %collective-permute-done.21.refs_3_, ...), custom_call_target="tpu_custom_call" | custom-call | flops 1000 | bytes 3501000 | tf_op jit(solution)/shard_map/pallas_call | solution.py:83
  (30 shorter events, 0.1 us)
Async XLA Ops:
  0.0 1.2 %copy-start = (bf16[256,2048]{1,0:T(8,128)(2,1)S(1)}, bf16[256,2048]{1,0:T(8,128)(2,1)}, u32[]{:S(2)}) copy-start(bf16[256,2048]{1,0:T(8,128)(2,1)} %x.1) | copy-start | bytes 3145732
  1.2 0.7 copy-start.5
  1.9 0.9 %copy-start.2 = (bf16[1024,128]{1,0:T(8,128)(2,1)S(1)}, bf16[1024,128]{1,0:T(8,128)(2,1)}, u32[]{:S(2)}) copy-start(bf16[1024,128]{1,0:T(8,128)(2,1)} %refs_0_) | copy-start | bytes 786436
  1.9 5.0 %copy-start.1 = (bf16[128,3072]{1,0:T(8,128)(2,1)S(1)}, bf16[128,3072]{1,0:T(8,128)(2,1)}, u32[]{:S(2)}) copy-start(bf16[128,3072]{1,0:T(8,128)(2,1)} %w) | copy-start | bytes 2359300
  2.8 10.6 %collective-permute-start.1 = (bf16[1024,128]{1,0:T(8,128)(2,1)S(1)}, bf16[1024,128]{1,0:T(8,128)(2,1)}, u32[]{:S(2)}, u32[]{:S(2)}) collective-permute-start(bf16[1024,128]{1,0:T(8,128)(2,1)S(1)} %copy-done.2), channel_id=1, source_target_pairs={{0,8},{1,9},{2,10},{3,11},{8,12},{9,13},{10,14},{11,15},{12,4},{13... | collective-permute-start | bytes 786440 | tf_op jit(solution)/shard_map/ppermute | solution.py:39
  7.0 6.4 %collective-permute-start = (bf16[128,768]{1,0:T(8,128)(2,1)S(1)}, bf16[128,768]{1,0:T(8,128)(2,1)S(1)}, u32[]{:S(2)}, u32[]{:S(2)}) collective-permute-start(bf16[128,768]{1,0:T(8,128)(2,1)S(1)} %get-tuple-element.33), channel_id=1, source_target_pairs={{0,2},{1,3},{2,0},{3,1},{4,6},{5,7},{6,4},{7,5},{8,10},{9,11},{10,... | collective-permute-start | bytes 589832 | tf_op jit(solution)/shard_map/ppermute | solution.py:45
  8.6 25.7 %collective-permute-start.10 = (bf16[272,2048]{1,0:T(8,128)(2,1)S(1)}, bf16[272,2048]{1,0:T(8,128)(2,1)S(1)}, u32[]{:S(2)}, u32[]{:S(2)}) collective-permute-start(bf16[272,2048]{1,0:T(8,128)(2,1)S(1)} %shard_map.55.refs_8_), channel_id=1, source_target_pairs={{0,16},{1,17},{2,18},{3,19},{4,20},{5,21},{6,22},{7,23},{8,24},{9,... | collective-permute-start | bytes 3342344 | tf_op jit(solution)/shard_map/ppermute | solution.py:51
  13.4 25.2 %collective-permute-start.9 = (bf16[272,2048]{1,0:T(8,128)(2,1)S(1)}, bf16[272,2048]{1,0:T(8,128)(2,1)S(1)}, u32[]{:S(2)}, u32[]{:S(2)}) collective-permute-start(bf16[272,2048]{1,0:T(8,128)(2,1)S(1)} %shard_map.55.refs_8_), channel_id=1, source_target_pairs={{0,2},{1,3},{2,0},{3,1},{4,6},{5,7},{6,4},{7,5},{8,10},{9,11},{10,... | collective-permute-start | bytes 3342344 | tf_op jit(solution)/shard_map/ppermute | solution.py:45
  15.7 12.4 %collective-permute-start.2 = (bf16[256,768]{1,0:T(8,128)(2,1)}, bf16[256,768]{1,0:T(8,128)(2,1)}, u32[]{:S(2)}, u32[]{:S(2)}) collective-permute-start(bf16[256,768]{1,0:T(8,128)(2,1)} %bitcast.refs_0_), channel_id=1, source_target_pairs={{0,8},{1,9},{2,10},{3,11},{8,12},{9,13},{10,14},{11,15},{12,4},{13... | collective-permute-start | bytes 1179656 | tf_op jit(solution)/shard_map/ppermute | solution.py:39
  18.2 35.0 %copy-start.3 = (bf16[1024,128]{1,0:T(8,128)(2,1)S(1)}, bf16[1024,128]{1,0:T(8,128)(2,1)}, u32[]{:S(2)}) copy-start(bf16[1024,128]{1,0:T(8,128)(2,1)} %refs_0_) | copy-start | bytes 786436
  18.2 20.6 %collective-permute-start.5 = (bf16[256,768]{1,0:T(8,128)(2,1)}, bf16[256,768]{1,0:T(8,128)(2,1)S(1)}, u32[]{:S(2)}, u32[]{:S(2)}) collective-permute-start(bf16[256,768]{1,0:T(8,128)(2,1)} %bitcast.refs_0_), channel_id=1, source_target_pairs={{0,1},{1,0},{2,3},{3,2},{4,5},{5,4},{6,7},{7,6},{8,9},{9,8},{10,11... | collective-permute-start | bytes 1179656 | tf_op jit(solution)/shard_map/ppermute | solution.py:45
  18.2 20.6 %collective-permute-start.11 = (bf16[1024,128]{1,0:T(8,128)(2,1)}, bf16[1024,128]{1,0:T(8,128)(2,1)S(1)}, u32[]{:S(2)}, u32[]{:S(2)}) collective-permute-start(bf16[1024,128]{1,0:T(8,128)(2,1)} %collective-permute-done.1.refs_1_.refs_0_), channel_id=1, source_target_pairs={{0,8},{1,9},{2,10},{3,11},{8,12},{9,13},{10,14},{11,15},{12,4},{13... | collective-permute-start | bytes 786440 | tf_op jit(solution)/shard_map/ppermute | solution.py:39
  28.1 11.7 %collective-permute-start.3 = (bf16[256,768]{1,0:T(8,128)(2,1)}, bf16[256,768]{1,0:T(8,128)(2,1)S(1)}, u32[]{:S(2)}, u32[]{:S(2)}) collective-permute-start(bf16[256,768]{1,0:T(8,128)(2,1)} %collective-permute-done.2.refs_1_), channel_id=1, source_target_pairs={{0,8},{1,9},{2,10},{3,11},{8,12},{9,13},{10,14},{11,15},{12,4},{13... | collective-permute-start | bytes 1179656 | tf_op jit(solution)/shard_map/ppermute | solution.py:39
  34.3 5.5 %collective-permute-start.6 = (bf16[256,768]{1,0:T(8,128)(2,1)}, bf16[256,768]{1,0:T(8,128)(2,1)S(1)}, u32[]{:S(2)}, u32[]{:S(2)}) collective-permute-start(bf16[256,768]{1,0:T(8,128)(2,1)} %collective-permute-done.2.refs_1_), channel_id=1, source_target_pairs={{0,1},{1,0},{2,3},{3,2},{4,5},{5,4},{6,7},{7,6},{8,9},{9,8},{10,11... | collective-permute-start | bytes 1179656 | tf_op jit(solution)/shard_map/ppermute | solution.py:45
  39.8 15.5 %collective-permute-start.12 = (bf16[272,2048]{1,0:T(8,128)(2,1)S(1)}, bf16[272,2048]{1,0:T(8,128)(2,1)S(1)}, u32[]{:S(2)}, u32[]{:S(2)}) collective-permute-start(bf16[272,2048]{1,0:T(8,128)(2,1)S(1)} %broadcast_select_fusion), channel_id=1, source_target_pairs={{0,16},{1,3},{2,18},{3,1},{4,20},{5,7},{6,22},{7,5},{8,24},{9,11},... | collective-permute-start | bytes 3342344 | tf_op jit(solution)/shard_map/ppermute | solution.py:61
  41.3 8.6 %collective-permute-start.4 = (bf16[256,768]{1,0:T(8,128)(2,1)S(1)}, bf16[256,768]{1,0:T(8,128)(2,1)S(1)}, u32[]{:S(2)}, u32[]{:S(2)}) collective-permute-start(bf16[256,768]{1,0:T(8,128)(2,1)S(1)} %collective-permute-done.3.refs_2_), channel_id=1, source_target_pairs={{0,8},{1,9},{2,10},{3,11},{8,12},{9,13},{10,14},{11,15},{12,4},{13... | collective-permute-start | bytes 1179656 | tf_op jit(solution)/shard_map/ppermute | solution.py:39
  44.6 9.9 %collective-permute-start.7 = (bf16[256,768]{1,0:T(8,128)(2,1)S(1)}, bf16[256,768]{1,0:T(8,128)(2,1)S(1)}, u32[]{:S(2)}, u32[]{:S(2)}) collective-permute-start(bf16[256,768]{1,0:T(8,128)(2,1)S(1)} %collective-permute-done.3.refs_2_), channel_id=1, source_target_pairs={{0,1},{1,0},{2,3},{3,2},{4,5},{5,4},{6,7},{7,6},{8,9},{9,8},{10,11... | collective-permute-start | bytes 1179656 | tf_op jit(solution)/shard_map/ppermute | solution.py:45
  49.9 4.7 %collective-permute-start.8 = (bf16[256,768]{1,0:T(8,128)(2,1)S(1)}, bf16[256,768]{1,0:T(8,128)(2,1)S(1)}, u32[]{:S(2)}, u32[]{:S(2)}) collective-permute-start(bf16[256,768]{1,0:T(8,128)(2,1)S(1)} %collective-permute-done.4.refs_3_), channel_id=1, source_target_pairs={{0,1},{1,0},{2,3},{3,2},{4,5},{5,4},{6,7},{7,6},{8,9},{9,8},{10,11... | collective-permute-start | bytes 1179656 | tf_op jit(solution)/shard_map/ppermute | solution.py:45
  49.9 10.2 %collective-permute-start.22 = (bf16[1024,128]{1,0:T(8,128)(2,1)S(1)}, bf16[1024,128]{1,0:T(8,128)(2,1)S(1)}, u32[]{:S(2)}, u32[]{:S(2)}) collective-permute-start(bf16[1024,128]{1,0:T(8,128)(2,1)S(1)} %collective-permute-done.11.refs_2_.refs_1_), channel_id=1, source_target_pairs={{0,8},{1,9},{2,10},{3,11},{8,12},{9,13},{10,14},{11,15},{12,4},{13... | collective-permute-start | bytes 786440 | tf_op jit(solution)/shard_map/ppermute | solution.py:39
  53.2 8.4 %collective-permute-start.24 = (bf16[1024,128]{1,0:T(8,128)(2,1)S(1)}, bf16[1024,128]{1,0:T(8,128)(2,1)S(1)}, u32[]{:S(2)}, u32[]{:S(2)}) collective-permute-start(bf16[1024,128]{1,0:T(8,128)(2,1)S(1)} %copy-done.3), channel_id=1, source_target_pairs={{0,2},{1,3},{2,0},{3,1},{4,6},{5,7},{6,4},{7,5},{8,10},{9,11},{10,... | collective-permute-start | bytes 786440 | tf_op jit(solution)/shard_map/ppermute | solution.py:45
  61.1 10.2 %copy-start.4 = (s32[32]{0:T(128)S(1)}, s32[32]{0:T(128)}, u32[]{:S(2)}) copy-start(s32[32]{0:T(128)} %counts.3) | copy-start | bytes 388
  61.7 25.9 %collective-permute-start.26 = (bf16[3,1024,128]{2,1,0:T(8,128)(2,1)S(1)}, bf16[3,1024,128]{2,1,0:T(8,128)(2,1)S(1)}, u32[]{:S(2)}, u32[]{:S(2)}) collective-permute-start(bf16[3,1024,128]{2,1,0:T(8,128)(2,1)S(1)} %shard_map.62), channel_id=1, source_target_pairs={{0,2},{1,3},{2,0},{3,1},{4,6},{5,7},{6,4},{7,5},{8,10},{9,11},{10,... | collective-permute-start | bytes 2359304 | tf_op jit(solution)/shard_map/ppermute | solution.py:45
  62.9 1.5 %collective-permute-start.13 = (bf16[256,512]{1,0:T(8,128)(2,1)S(1)}, bf16[256,512]{1,0:T(8,128)(2,1)S(1)}, u32[]{:S(2)}, u32[]{:S(2)}) collective-permute-start(bf16[256,512]{1,0:T(8,128)(2,1)S(1)} %get-tuple-element.40.refs_2_), channel_id=1, source_target_pairs={{0,1},{1,0},{2,3},{3,2},{4,5},{5,4},{6,7},{7,6},{8,9},{9,8},{10,11... | collective-permute-start | bytes 786440 | tf_op jit(solution)/shard_map/ppermute | solution.py:45
  62.9 2.2 %collective-permute-start.14 = (bf16[256,512]{1,0:T(8,128)(2,1)S(1)}, bf16[256,512]{1,0:T(8,128)(2,1)S(1)}, u32[]{:S(2)}, u32[]{:S(2)}) collective-permute-start(bf16[256,512]{1,0:T(8,128)(2,1)S(1)} %get-tuple-element.41.refs_3_), channel_id=1, source_target_pairs={{0,1},{1,0},{2,3},{3,2},{4,5},{5,4},{6,7},{7,6},{8,9},{9,8},{10,11... | collective-permute-start | bytes 786440 | tf_op jit(solution)/shard_map/ppermute | solution.py:45
  63.5 3.4 %collective-permute-start.15 = (bf16[256,512]{1,0:T(8,128)(2,1)S(1)}, bf16[256,512]{1,0:T(8,128)(2,1)S(1)}, u32[]{:S(2)}, u32[]{:S(2)}) collective-permute-start(bf16[256,512]{1,0:T(8,128)(2,1)S(1)} %get-tuple-element.42.refs_4_), channel_id=1, source_target_pairs={{0,1},{1,0},{2,3},{3,2},{4,5},{5,4},{6,7},{7,6},{8,9},{9,8},{10,11... | collective-permute-start | bytes 786440 | tf_op jit(solution)/shard_map/ppermute | solution.py:45
  63.5 7.8 %collective-permute-start.16 = (bf16[256,512]{1,0:T(8,128)(2,1)S(1)}, bf16[256,512]{1,0:T(8,128)(2,1)S(1)}, u32[]{:S(2)}, u32[]{:S(2)}) collective-permute-start(bf16[256,512]{1,0:T(8,128)(2,1)S(1)} %get-tuple-element.43.refs_5_), channel_id=1, source_target_pairs={{0,1},{1,0},{2,3},{3,2},{4,5},{5,4},{6,7},{7,6},{8,9},{9,8},{10,11... | collective-permute-start | bytes 786440 | tf_op jit(solution)/shard_map/ppermute | solution.py:45
  64.5 6.8 %collective-permute-start.17 = (bf16[256,512]{1,0:T(8,128)(2,1)S(1)}, bf16[256,512]{1,0:T(8,128)(2,1)S(1)}, u32[]{:S(2)}, u32[]{:S(2)}) collective-permute-start(bf16[256,512]{1,0:T(8,128)(2,1)S(1)} %get-tuple-element.44), channel_id=1, source_target_pairs={{1,4},{3,6},{4,1},{5,8},{6,3},{7,10},{8,5},{9,12},{10,7},{11,14},{... | collective-permute-start | bytes 786440 | tf_op jit(solution)/shard_map/ppermute | solution.py:67
  65.2 8.8 %collective-permute-start.19 = (bf16[256,512]{1,0:T(8,128)(2,1)S(1)}, bf16[256,512]{1,0:T(8,128)(2,1)S(1)}, u32[]{:S(2)}, u32[]{:S(2)}) collective-permute-start(bf16[256,512]{1,0:T(8,128)(2,1)S(1)} %get-tuple-element.48), channel_id=1, source_target_pairs={{1,4},{3,6},{4,1},{5,8},{6,3},{7,10},{8,5},{9,12},{10,7},{11,14},{... | collective-permute-start | bytes 786440 | tf_op jit(solution)/shard_map/ppermute | solution.py:67
  66.9 23.4 %collective-permute-start.23 = (bf16[4,1024,128]{2,1,0:T(8,128)(2,1)S(1)}, bf16[4,1024,128]{2,1,0:T(8,128)(2,1)S(1)}, u32[]{:S(2)}, u32[]{:S(2)}) collective-permute-start(bf16[4,1024,128]{2,1,0:T(8,128)(2,1)S(1)} %shard_map.61.refs_4_), channel_id=1, source_target_pairs={{0,1},{1,0},{2,3},{3,2},{4,5},{5,4},{6,7},{7,6},{8,9},{9,8},{10,11... | collective-permute-start | bytes 3145736 | tf_op jit(solution)/shard_map/ppermute | solution.py:45
  76.6 5.6 %collective-permute-start.20 = (bf16[256,256]{1,0:T(8,128)(2,1)S(1)}, bf16[256,256]{1,0:T(8,128)(2,1)S(1)}, u32[]{:S(2)}, u32[]{:S(2)}) collective-permute-start(bf16[256,256]{1,0:T(8,128)(2,1)S(1)} %get-tuple-element.49), channel_id=1, source_target_pairs={{0,16},{1,17},{2,18},{3,19},{4,20},{5,21},{6,22},{7,23},{8,24},{9,... | collective-permute-start | bytes 393224 | tf_op jit(solution)/shard_map/ppermute | solution.py:51
  78.1 7.3 %collective-permute-start.21 = (bf16[256,256]{1,0:T(8,128)(2,1)S(1)}, bf16[256,256]{1,0:T(8,128)(2,1)S(1)}, u32[]{:S(2)}, u32[]{:S(2)}) collective-permute-start(bf16[256,256]{1,0:T(8,128)(2,1)S(1)} %get-tuple-element.50), channel_id=1, source_target_pairs={{0,18},{1,19},{2,16},{3,17},{4,22},{5,23},{6,20},{7,21},{8,26},{9,... | collective-permute-start | bytes 393224 | tf_op jit(solution)/shard_map/ppermute | solution.py:51
  78.9 8.8 %collective-permute-start.18 = (bf16[256,256]{1,0:T(8,128)(2,1)S(1)}, bf16[256,256]{1,0:T(8,128)(2,1)S(1)}, u32[]{:S(2)}, u32[]{:S(2)}) collective-permute-start(bf16[256,256]{1,0:T(8,128)(2,1)S(1)} %get-tuple-element.46), channel_id=1, source_target_pairs={{0,2},{1,3},{2,0},{3,1},{4,6},{5,7},{6,4},{7,5},{8,10},{9,11},{10,... | collective-permute-start | bytes 393224 | tf_op jit(solution)/shard_map/ppermute | solution.py:45
  87.6 2.7 %collective-permute-start.27 = (bf16[3,1024,128]{2,1,0:T(8,128)(2,1)S(1)}, bf16[3,1024,128]{2,1,0:T(8,128)(2,1)S(1)}, u32[]{:S(2)}, u32[]{:S(2)}) collective-permute-start(bf16[3,1024,128]{2,1,0:T(8,128)(2,1)S(1)} %collective-permute-done.26.refs_8_), channel_id=1, source_target_pairs={{0,1},{1,0},{2,3},{3,2},{4,5},{5,4},{6,7},{7,6},{8,9},{9,8},{10,11... | collective-permute-start | bytes 2359304 | tf_op jit(solution)/shard_map/ppermute | solution.py:45
  87.9 2.4 %collective-permute-start.25 = (bf16[1024,128]{1,0:T(8,128)(2,1)S(1)}, bf16[1024,128]{1,0:T(8,128)(2,1)S(1)}, u32[]{:S(2)}, u32[]{:S(2)}) collective-permute-start(bf16[1024,128]{1,0:T(8,128)(2,1)S(1)} %collective-permute-done.24.refs_6_), channel_id=1, source_target_pairs={{0,1},{1,0},{2,3},{3,2},{4,5},{5,4},{6,7},{7,6},{8,9},{9,8},{10,11... | collective-permute-start | bytes 786440 | tf_op jit(solution)/shard_map/ppermute | solution.py:45

commit v2 on v1

--- a/solution.py
+++ b/solution.py
@@ -11,7 +11,7 @@
 PAIR = 2 * HD
 VMEM = pl.BlockSpec(memory_space=pltpu.VMEM)
 SMEM = pl.BlockSpec(memory_space=pltpu.SMEM)
-HBM = pl.BlockSpec(memory_space=pltpu.HBM)
+ANY = pl.BlockSpec(memory_space=pl.ANY)
 MARK = 16
 BF16 = jnp.bfloat16
 F32 = jnp.float32
@@ -77,14 +77,16 @@
     return lax.optimization_barrier((x,) + others)[0]
 
 
-def call(body, shapes, args, specs=None, scratch=(), limit=16, cost=0.0):
+def call(body, shapes, args, specs=None, out_spec=VMEM, scratch=(), limit=16, cost=0.0):
     many = isinstance(shapes, list)
-    outs = [jax.ShapeDtypeStruct(s, BF16) for s in (shapes if many else [shapes])]
+    outs = shapes if many else [shapes]
+    outs = [s if isinstance(s[0], tuple) else (s, BF16) for s in outs]
+    outs = [jax.ShapeDtypeStruct(*s) for s in outs]
     return pl.pallas_call(
         body,
         out_shape=outs if many else outs[0],
         in_specs=specs or [VMEM] * len(args),
-        out_specs=[VMEM] * len(outs) if many else VMEM,
+        out_specs=[VMEM] * len(outs) if many else out_spec,
         scratch_shapes=list(scratch),
         compiler_params=pltpu.CompilerParams(vmem_limit_bytes=limit * 1024 * 1024),
         cost_estimate=pl.CostEstimate(
@@ -125,33 +127,53 @@
         refs[-1][n] = ref[...]
 
 
-def stack(arrays):
-    return call(stack_body, (len(arrays),) + arrays[0].shape, arrays, limit=8)
-
-
-def gather_weight(pieces, weight, count):
+def stack(arrays, **options):
+    return call(stack_body, (len(arrays),) + arrays[0].shape, arrays, limit=8, **options)
+
+
+def gather_weight(piece, piece_next, weight):
     _, y, core = place()
-    rows = pieces[0].shape[0] // 2
-    for n, piece in enumerate(pieces):
-        which_core = 1 - core if n // count else core
+    rows = piece.shape[0] // 2
+    for held, which_core in ((piece, core), (piece_next, 1 - core)):
         for half, which_y in ((0, y), (1, 1 - y)):
-            into = 4 * ring_source(n % count, count) + 2 * which_y + which_core
-            into = pl.ds(pl.multiple_of(into * rows, 16), rows)
-            weight[into, :] = piece[half * rows : (half + 1) * rows, :]
+            into = pl.ds(pl.multiple_of((2 * which_y + which_core) * rows, 16), rows)
+            weight[into, :] = held[half * rows : (half + 1) * rows, :]
+
+
+def project(block, weight, step, count):
+    rows = weight.shape[0]
+    columns = pl.ds(pl.multiple_of(ring_source(step, count) * rows, HD), rows)
+    return jnp.dot(block[MARK:, columns], weight[...], preferred_element_type=F32)
 
 
 def project_body(count, *refs):
-    pieces, blocks = refs[: 2 * count], refs[2 * count : 2 * count + 4]
-    q, marks, *kv, halo, halo_across, weight = refs[2 * count + 4 :]
-    gather_weight(pieces, weight, count)
+    steps = count - 1
+    pieces, blocks, (total, weights) = refs[: 2 * steps], refs[2 * steps : 2 * steps + 3], refs[-2:]
+    for step in range(steps):
+        gather_weight(pieces[step], pieces[steps + step], weights.at[step])
     for n, block in enumerate(blocks):
-        done = jnp.dot(block[MARK:, :], weight[...], preferred_element_type=F32).astype(BF16)
+        done = [project(block, weights.at[step], step, count) for step in range(steps)]
+        total[n] = functools.reduce(lambda a, b: a + b, done)
+
+
+def project_last_body(count, *refs):
+    piece, piece_next, total, weights, *blocks = refs[:8]
+    q, marks, *kv, halo, halo_across, weight = refs[8:]
+    gather_weight(piece, piece_next, weight)
+    for n, block in enumerate(blocks):
+        done = project(block, weight, count - 1, count)
+        if n < 3:
+            done = done + total[n]
+        else:
+            for step in range(count - 1):
+                done = done + project(block, weights.at[step], step, count)
+        done = done.astype(BF16)
         q[n] = done[:, :PAIR]
-        kv[n][...] = done[:, PAIR:]
+        kv[n // 2][n % 2] = done[:, PAIR:]
         marks[n] = block[:MARK, :HD]
     _, y, core = place()
-    halo[...] = jnp.where(y == core, kv[0][...], kv[1][...])
-    halo_across[...] = jnp.where(y == core, kv[2][...], kv[3][...])
+    halo[...] = jnp.where(y == core, kv[0][0], kv[0][1])
+    halo_across[...] = jnp.where(y == core, kv[1][0], kv[1][1])
 
 
 def attend(q, keys_values):
@@ -171,26 +193,35 @@
     return (context / total).astype(BF16)
 
 
-def attend_body(blocks, wider, counts, *refs):
-    q, marks, kv, other, halo = *refs[:2], refs[2:6], refs[6:10], refs[10:12]
-    beyond, outs, far = refs[12:16], refs[-1 - len(blocks) : -1], refs[-1]
+def attend_body(edge, wider, counts, q, marks, kv, kv_across, other, other_across, *refs):
+    halo, refs = (refs[:2], refs[2:]) if edge else ((), refs)
+    beyond, outs = refs[: 4 * wider], refs[4 * wider :]
+    kv, other = (kv, kv_across), (other, other_across)
     side, y, core = place()
     inner = lax.axis_size("inner")
-    for b, out in zip(blocks, outs):
-        which_side, which_y = lax.rem(side + b // 2, 2), lax.rem(y + b % 2, 2)
+    n = lax.rem(y + core + 1 - edge, 2)
+    which_y = lax.rem(y + n, 2)
+    for p in range(2):
+        which_side = lax.rem(side + p, 2)
         number = (lax.axis_index("outer") - side + which_side) * inner
         number = number + lax.axis_index("inner") - 2 * y + 2 * which_y
-        far[...] = jnp.where(which_y == core, halo[b // 2][...], other[b ^ 1][...])
-        mark = marks[b, 0:1, :].astype(F32)
-        slots = [mark[:, n : n + 1] for n in range(5)]
+        mark = marks[2 * p + n, 0:1, :].astype(F32)
+        slots = [mark[:, k : k + 1] for k in range(5)]
+        far = halo[p] if edge else other[p].at[1 - n]
         sources = [
-            (kv[b], slots[0], number),
-            (kv[b ^ 2], jnp.where(which_side == 0, slots[2], slots[1]), number + inner * (1 - 2 * which_side)),
-            (other[b], jnp.where(core == 0, slots[4], slots[3]), number + 1 - 2 * core),
+            (kv[p].at[n], slots[0], number),
+            (
+                kv[1 - p].at[n],
+                jnp.where(which_side == 0, slots[2], slots[1]),
+                number + inner * (1 - 2 * which_side),
+            ),
+            (other[p].at[n], jnp.where(core == 0, slots[4], slots[3]), number + 1 - 2 * core),
             (far, jnp.where(core == 0, slots[3], slots[4]), number - 1 + 2 * core),
         ]
         if wider:
-            far_outer = jnp.where(which_side == 0, beyond[b % 2][...], beyond[2 + b % 2][...])
+            far_outer = beyond[0][...]
+            for k in range(1, 4):
+                far_outer = jnp.where(2 * which_side + n == k, beyond[k][...], far_outer)
             mark_outer = jnp.where(which_side == 0, slots[1], slots[2])
             sources.append((far_outer, mark_outer, number - inner * (1 - 2 * which_side)))
         for head in range(2):
@@ -202,29 +233,44 @@
                 keys_values.append(
                     (source[:, at : at + HD], source[:, PAIR + at : PAIR + at + HD], length)
                 )
-            out[:, at : at + HD] = attend(q[b, :, at : at + HD], keys_values)
+            outs[p][:, at : at + HD] = attend(q[2 * p + n, :, at : at + HD], keys_values)
+
+
+def attend_edge_body(wider, *refs):
+    inner_0, inner_1, outs, (edge_0, edge_1) = *refs[:2], refs[-6:-2], refs[-2:]
+    attend_body(1, wider, *refs[2:-6], edge_0, edge_1)
+    _, y, core = place()
+    for b, out in enumerate(outs):
+        done, edge = (inner_1, edge_1) if b // 2 else (inner_0, edge_0)
+        out[...] = jnp.where(lax.rem(y + core, 2) == b % 2, edge[...], done[...])
 
 
 def finish_body(count, *refs):
     contexts, refs = refs[:4], refs[4:]
-    out, context = refs[-2:]
-    bundles = refs[:-2]
+    out, context, tiles, sems = refs[-4:]
+    bundles = refs[:-4]
     side, y, core = place()
+    copies = []
     for b, piece in enumerate(contexts):
         pair = 2 * lax.rem(side + b // 2, 2) + lax.rem(y + b % 2, 2)
         context[pair] = piece[...]
     whole = jnp.concatenate([context[pair] for pair in range(4)], axis=1)
-    here, here_next, *there = bundles
     for step in range(count):
-        z = ring_source(step, count)
-        pair = (there[0][...], there[1][...]) if step == 0 else (there[2][step - 1], there[3][step - 1])
-        for which_y, mine, other in ((y, here[step], here_next[step]), (1 - y, *pair)):
+        at, n = (4, 0) if step == count - 1 else (0, step)
+        for which_y, k in ((y, 0), (1 - y, 2)):
+            mine, other = bundles[at + k][n], bundles[at + k + 1][n]
             tile = jnp.concatenate(
                 [jnp.where(core == 0, mine, other), jnp.where(core == 0, other, mine)], axis=1
             )
-            column = pl.multiple_of((4 * z + 2 * which_y) * HD, HD)
+            column = pl.multiple_of((4 * ring_source(step, count) + 2 * which_y) * HD, HD)
             done = jnp.dot(whole, tile, preferred_element_type=F32)
-            out[:, pl.ds(column, PAIR)] = done.astype(BF16)
+            m = len(copies)
+            tiles[m] = done.astype(BF16)
+            into = out.at[:, pl.ds(column, PAIR)]
+            copies.append(pltpu.make_async_copy(tiles.at[m], into, sems.at[m]))
+            copies[-1].start()
+    for copy in copies:
+        copy.wait()
 
 
 def per_device(tokens, w_qkv, w_out, neighbours, counts):
@@ -236,22 +282,23 @@
     w_rows = w_qkv.shape[0]
     side, _, core = place()
 
-    normed = call(norm_body, (MARK + rows, width), [tokens, neighbours], limit=8)
     mine, send = call(
         pick_body,
         [(w_rows, wide)] * 2,
-        [after(w_qkv, normed)],
-        specs=[pl.BlockSpec(memory_space=pl.ANY)],
+        [w_qkv],
+        specs=[ANY],
         scratch=[pltpu.SemaphoreType.DMA((6,))],
         limit=8,
     )
+    normed = call(norm_body, (MARK + rows, width), [after(tokens, send), neighbours], limit=8)
     block_x = swap(normed, 4)
     got = swap(send, 2)
     strips = [w_out]
     if count > 1:
-        strips.append(along_ring(after(w_out, normed)))
-    block_y = swap(after(normed, got, *strips[1:]), 2)
-    pieces = [stack([mine, after(got, *strips[1:])]).reshape(2 * w_rows, wide)]
+        strips.append(along_ring(after(w_out, send)))
+    piece = stack([mine, got], cost=1.0).reshape(2 * w_rows, wide)
+    block_y = swap(after(normed, piece, *strips[1:]), 2)
+    pieces = [after(piece, *strips[1:])]
     for _ in range(count - 1):
         pieces.append(along_ring(pieces[-1]))
     next_pieces = [swap(p, 1) for p in pieces]
@@ -262,50 +309,65 @@
     block_d = swap_by_core(block_d, 4, 2)
     for n in range(len(strips), count):
         strips.append(along_ring(after(strips[-1], pieces[-1])))
-    there = [swap(after(w_out, pieces[-1]), 2)]
-    pieces = pieces + next_pieces
-
+    here = stack([after(strips[0], pieces[-1])] + strips[1:-1])
+    there = swap(here, 2)
+    total, weights = call(
+        functools.partial(project_body, count),
+        [((3, rows, wide), F32), (count - 1, 4 * w_rows, wide)],
+        pieces[:-1] + next_pieces[:-1] + [normed, block_y, block_x],
+        cost=3.0,
+    )
     q, marks, *kv, halo, halo_across = call(
-        functools.partial(project_body, count),
-        [(4, rows, PAIR), (4, MARK, HD)] + [(rows, 2 * PAIR)] * 6,
-        pieces + [normed, block_y, block_x, block_d],
-        scratch=[pltpu.VMEM((width, wide), BF16)],
+        functools.partial(project_last_body, count),
+        [(4, rows, PAIR), (4, MARK, HD)] + [(2, rows, 2 * PAIR)] * 2 + [(rows, 2 * PAIR)] * 2,
+        [pieces[-1], next_pieces[-1], total, weights, normed, block_y, block_x, block_d],
+        scratch=[pltpu.VMEM((4 * w_rows, wide), BF16)],
         cost=5.0,
     )
-    here = stack([after(strips[0], halo)] + strips[1:])
-    here_next = swap(here, 1)
-    if count > 1:
-        there.append(swap(after(stack([after(strips[1], halo)] + strips[2:]), there[0]), 2))
     halo, halo_across = to_next_group(halo), to_next_group(halo_across)
-    next_kv = [swap(b, 1) for b in kv]
+    next_kv = [swap(after(b, strips[-1]), 1) for b in kv]
+    here_last = after(strips[-1], next_kv[0])
+    there_last = swap(here_last, 2)
+    here_next, here_last_next = swap(after(here, next_kv[0]), 1), swap(here_last, 1)
     beyond = []
     if wider:
-        upper = [jnp.where(side == 1, kv[b], kv[b + 2]) for b in range(2)]
-        lower = [jnp.where(side == 0, kv[b], kv[b + 2]) for b in range(2)]
+        upper = [jnp.where(side == 1, kv[0][b], kv[1][b]) for b in range(2)]
+        lower = [jnp.where(side == 0, kv[0][b], kv[1][b]) for b in range(2)]
         beyond = [along_outer(b, 2) for b in upper] + [along_outer(b, -2) for b in lower]
 
-    def attended(blocks, halo, halo_across):
-        held = [counts, q, marks] + kv + next_kv + [halo, halo_across] + beyond
-        return call(
-            functools.partial(attend_body, blocks, wider),
-            [(rows, PAIR)] * len(blocks),
-            held,
-            specs=[SMEM] + [VMEM] * (len(held) - 1),
-            scratch=[pltpu.VMEM((rows, 2 * PAIR), BF16)],
-            cost=2.5,
-        )
-
-    c_1, c_0 = attended((1, 0), halo, halo)
-    c_3, c_2 = attended((3, 2), after(halo, c_1), halo_across)
+    held = [counts, q, marks] + kv + next_kv
+    context = (rows, PAIR)
+    inside = call(
+        functools.partial(attend_body, 0, wider),
+        [context] * 2,
+        held + beyond,
+        specs=[SMEM] + [VMEM] * (len(held + beyond) - 1),
+        cost=4.0,
+    )
+    held = list(inside) + held + [halo, halo_across] + beyond
+    c_0, c_1, c_2, c_3 = call(
+        functools.partial(attend_edge_body, wider),
+        [context] * 4,
+        held,
+        specs=[VMEM] * 2 + [SMEM] + [VMEM] * (len(held) - 3),
+        scratch=[pltpu.VMEM(context, BF16)] * 2,
+        cost=4.0,
+    )
     contexts = [c_0, swap(c_1, 2), swap(c_2, 4), swap(c_3, 6)]
-    there_next = swap(after(there[1], *contexts[1:]), 1) if count > 1 else None
-    bundles = [here, here_next, there[0], swap(there[0], 1)]
-    bundles += [there[1], there_next] if count > 1 else []
+    there_next = swap(after(there, there_last, *contexts[1:]), 1)
+    there_last_next = swap(there_last, 1)
+    bundles = [here, here_next, there, there_next]
+    bundles += [b[None] for b in (here_last, here_last_next, there_last, there_last_next)]
     return call(
         functools.partial(finish_body, count),
         (rows, width),
         contexts + bundles,
-        scratch=[pltpu.VMEM((4, rows, PAIR), BF16)],
+        out_spec=ANY,
+        scratch=[
+            pltpu.VMEM((4, rows, PAIR), BF16),
+            pltpu.VMEM((2 * count, rows, PAIR), BF16),
+            pltpu.SemaphoreType.DMA((2 * count,)),
+        ],
         cost=1.0,
     )
 

time: 93 us -> 88.9 us (0.956)
  starting transfers between devices: 36.7 us -> 33.4 us
  Pallas kernels: 15.9 us -> 14.9 us
    ppermute x16 -> x15, waiting for transfers between devices: 13.2 us -> 15.7 us  [swap(): return lax.ppermute(x, 'inner', [(i, i ^ r) for i in range(inner)])]
    ppermute x3, waiting for transfers between devices: 8.16 us -> 5.79 us  [swap(): return lax.ppermute(x, ('outer', 'inner'), pairs)]
    ppermute x16 -> x15, starting transfers between devices: 12.8 us -> 10.5 us  [swap(): return lax.ppermute(x, 'inner', [(i, i ^ r) for i in range(inner)])]
    ppermute x6, starting transfers between devices: 17.2 us -> 15.9 us  [along_ring(): return lax.ppermute(x, 'inner', pairs)]
    pallas_call x9, Pallas kernels: 15.9 us -> 14.9 us  [call(): pl.pallas_call(body, out_shape=outs if many else outs[0], in_specs=specs...]
    unnamed x12 -> x10, local copies, waits for them, and re-layouts: 2.22 us -> 3.02 us
  transfers between devices with their start and end apart: 28 -> 27, of which waited for: 13 -> 9; matrix products, arithmetic and copies ran while one was open for 0% -> 0% of each run, Pallas kernels for 14% -> 14%
where the time goes in v2:
time: 88.9 us; the launch traced here: 88.7 us
  waiting for transfers between devices  37.1 us (42%)
  starting transfers between devices  33.4 us (38%)
  Pallas kernels  14.9 us (17%)
  local copies, waits for them, and re-layouts  3.02 us (3%)
    ppermute x6, starting transfers between devices, along_ring(): return lax.ppermute(x, 'inner', pairs)  15.9 us
    ppermute x15, waiting for transfers between devices, swap(): return lax.ppermute(x, 'inner', [(i, i ^ r) for i in range(inner)])  15.7 us
    ppermute x6, waiting for transfers between devices, along_ring(): return lax.ppermute(x, 'inner', pairs)  15.6 us
    pallas_call x9, Pallas kernels, call(): pl.pallas_call(body, out_shape=outs if many else outs[0], in_specs=specs...  14.9 us
    ppermute x15, starting transfers between devices, swap(): return lax.ppermute(x, 'inner', [(i, i ^ r) for i in range(inner)])  10.5 us
    ppermute x3, waiting for transfers between devices, swap(): return lax.ppermute(x, ('outer', 'inner'), pairs)  5.79 us
    ppermute x3, starting transfers between devices, swap(): return lax.ppermute(x, ('outer', 'inner'), pairs)  4.02 us
    unnamed x10, local copies, waits for them, and re-layouts  3.02 us
  transfers between devices with their start and end apart: 27, of which 9 were waited for; matrix products, arithmetic and copies ran while one was open for 0% of the time, Pallas kernels for 14%

profile of v2, /device:TPU:0, one launch (start us, length us, event | category | flops | bytes accessed | tf_op | source)
XLA Modules:
  0.0 88.7 jit_solution(5436081984863200429)
XLA Ops:
  0.0 1.1 %copy-done.1 = bf16[128,3072]{1,0:T(8,128)(2,1)S(1)} copy-done((bf16[128,3072]{1,0:T(8,128)(2,1)S(1)}, bf16[128,3072]{1,0:T(8,128)(2,1)}, u32[]{:S(2)}) %copy-start.1) | copy-done | bytes 786456
  1.1 0.1 shard_map.55
  1.3 4.1 %collective-permute-start.1 = (bf16[1024,128]{1,0:T(8,128)(2,1)}, bf16[1024,128]{1,0:T(8,128)(2,1)}, u32[]{:S(2)}, u32[]{:S(2)}) collective-permute-start(bf16[1024,128]{1,0:T(8,128)(2,1)} %refs_0_), channel_id=1, source_target_pairs={{0,8},{1,9},{2,10},{3,11},{8,12},{9,13},{10,14},{11,15},{12,4},{13... | collective-permute-start | bytes 786440 | tf_op jit(solution)/shard_map/ppermute | solution.py:39
  5.4 1.5 %collective-permute-start = (bf16[128,768]{1,0:T(8,128)(2,1)S(1)}, bf16[128,768]{1,0:T(8,128)(2,1)S(1)}, u32[]{:S(2)}, u32[]{:S(2)}) collective-permute-start(bf16[128,768]{1,0:T(8,128)(2,1)S(1)} %get-tuple-element.34), channel_id=1, source_target_pairs={{0,2},{1,3},{2,0},{3,1},{4,6},{5,7},{6,4},{7,5},{8,10},{9,11},{10,... | collective-permute-start | bytes 589832 | tf_op jit(solution)/shard_map/ppermute | solution.py:45
  6.9 1.2 %copy-done = bf16[256,2048]{1,0:T(8,128)(2,1)S(1)} copy-done((bf16[256,2048]{1,0:T(8,128)(2,1)S(1)}, bf16[256,2048]{1,0:T(8,128)(2,1)}, u32[]{:S(2)}) %copy-start) | copy-done | bytes 1048600
  8.1 0.7 copy-done.4
  8.8 0.6 shard_map.57.refs_6_.refs_4_
  9.4 1.6 %collective-permute-start.10 = (bf16[272,2048]{1,0:T(8,128)(2,1)S(1)}, bf16[272,2048]{1,0:T(8,128)(2,1)S(1)}, u32[]{:S(2)}, u32[]{:S(2)}) collective-permute-start(bf16[272,2048]{1,0:T(8,128)(2,1)S(1)} %shard_map.57.refs_6_.refs_4_), channel_id=1, source_target_pairs={{0,16},{1,17},{2,18},{3,19},{4,20},{5,21},{6,22},{7,23},{8,24},{9,... | collective-permute-start | bytes 3342344 | tf_op jit(solution)/shard_map/ppermute | solution.py:51
  10.9 0.8 collective-permute-done.refs_1_
  11.7 0.8 shard_map.56
  12.5 0.0 collective-permute-done.1.refs_1_
  12.5 1.5 %collective-permute-start.9 = (bf16[272,2048]{1,0:T(8,128)(2,1)S(1)}, bf16[272,2048]{1,0:T(8,128)(2,1)S(1)}, u32[]{:S(2)}, u32[]{:S(2)}) collective-permute-start(bf16[272,2048]{1,0:T(8,128)(2,1)S(1)} %shard_map.57.refs_6_.refs_4_), channel_id=1, source_target_pairs={{0,2},{1,3},{2,0},{3,1},{4,6},{5,7},{6,4},{7,5},{8,10},{9,11},{10,... | collective-permute-start | bytes 3342344 | tf_op jit(solution)/shard_map/ppermute | solution.py:45
  14.0 2.1 %collective-permute-start.2 = (bf16[256,768]{1,0:T(8,128)(2,1)}, bf16[256,768]{1,0:T(8,128)(2,1)}, u32[]{:S(2)}, u32[]{:S(2)}) collective-permute-start(bf16[256,768]{1,0:T(8,128)(2,1)} %bitcast.refs_0_), channel_id=1, source_target_pairs={{0,8},{1,9},{2,10},{3,11},{8,12},{9,13},{10,14},{11,15},{12,4},{13... | collective-permute-start | bytes 1179656 | tf_op jit(solution)/shard_map/ppermute | solution.py:39
  16.1 0.7 collective-permute-start.11
  16.8 9.6 %collective-permute-done.2.refs_1_ = bf16[256,768]{1,0:T(8,128)(2,1)} collective-permute-done((bf16[256,768]{1,0:T(8,128)(2,1)}, bf16[256,768]{1,0:T(8,128)(2,1)}, u32[]{:S(2)}, u32[]{:S(2)}) %collective-permute-start.2) | collective-permute-done | bytes 393248 | tf_op jit(solution)/shard_map/ppermute | solution.py:39
  26.4 3.0 %collective-permute-start.3 = (bf16[256,768]{1,0:T(8,128)(2,1)}, bf16[256,768]{1,0:T(8,128)(2,1)S(1)}, u32[]{:S(2)}, u32[]{:S(2)}) collective-permute-start(bf16[256,768]{1,0:T(8,128)(2,1)} %collective-permute-done.2.refs_1_), channel_id=1, source_target_pairs={{0,8},{1,9},{2,10},{3,11},{8,12},{9,13},{10,14},{11,15},{12,4},{13... | collective-permute-start | bytes 1179656 | tf_op jit(solution)/shard_map/ppermute | solution.py:39
  29.4 5.8 %collective-permute-done.10.refs_8_.refs_6_ = bf16[272,2048]{1,0:T(8,128)(2,1)S(1)} collective-permute-done((bf16[272,2048]{1,0:T(8,128)(2,1)S(1)}, bf16[272,2048]{1,0:T(8,128)(2,1)S(1)}, u32[]{:S(2)}, u32[]{:S(2)}) %collective-permute-start.10) | collective-permute-done | bytes 1114144 | tf_op jit(solution)/shard_map/ppermute | solution.py:51
  35.2 2.5 %collective-permute-done.9.refs_7_.refs_5_ = bf16[272,2048]{1,0:T(8,128)(2,1)S(1)} collective-permute-done((bf16[272,2048]{1,0:T(8,128)(2,1)S(1)}, bf16[272,2048]{1,0:T(8,128)(2,1)S(1)}, u32[]{:S(2)}, u32[]{:S(2)}) %collective-permute-start.9) | collective-permute-done | bytes 1114144 | tf_op jit(solution)/shard_map/ppermute | solution.py:45
  37.7 0.1 broadcast_select_fusion
  37.9 1.6 %collective-permute-start.12 = (bf16[272,2048]{1,0:T(8,128)(2,1)S(1)}, bf16[272,2048]{1,0:T(8,128)(2,1)S(1)}, u32[]{:S(2)}, u32[]{:S(2)}) collective-permute-start(bf16[272,2048]{1,0:T(8,128)(2,1)S(1)} %broadcast_select_fusion), channel_id=1, source_target_pairs={{0,16},{1,3},{2,18},{3,1},{4,20},{5,7},{6,22},{7,5},{8,24},{9,11},... | collective-permute-start | bytes 3342344 | tf_op jit(solution)/shard_map/ppermute | solution.py:61
  39.4 3.1 %collective-permute-start.4 = (bf16[256,768]{1,0:T(8,128)(2,1)S(1)}, bf16[256,768]{1,0:T(8,128)(2,1)S(1)}, u32[]{:S(2)}, u32[]{:S(2)}) collective-permute-start(bf16[256,768]{1,0:T(8,128)(2,1)S(1)} %collective-permute-done.3.refs_2_), channel_id=1, source_target_pairs={{0,8},{1,9},{2,10},{3,11},{8,12},{9,13},{10,14},{11,15},{12,4},{13... | collective-permute-start | bytes 1179656 | tf_op jit(solution)/shard_map/ppermute | solution.py:39
  42.5 6.0 %collective-permute-done.4.refs_0_ = bf16[256,768]{1,0:T(8,128)(2,1)S(1)} collective-permute-done((bf16[256,768]{1,0:T(8,128)(2,1)S(1)}, bf16[256,768]{1,0:T(8,128)(2,1)S(1)}, u32[]{:S(2)}, u32[]{:S(2)}) %collective-permute-start.4) | collective-permute-done | bytes 393248 | tf_op jit(solution)/shard_map/ppermute | solution.py:39
  48.5 3.0 %collective-permute-start.13 = (bf16[1024,128]{1,0:T(8,128)(2,1)S(1)}, bf16[1024,128]{1,0:T(8,128)(2,1)S(1)}, u32[]{:S(2)}, u32[]{:S(2)}) collective-permute-start(bf16[1024,128]{1,0:T(8,128)(2,1)S(1)} %collective-permute-done.11.refs_2_), channel_id=1, source_target_pairs={{0,8},{1,9},{2,10},{3,11},{8,12},{9,13},{10,14},{11,15},{12,4},{13... | collective-permute-start | bytes 786440 | tf_op jit(solution)/shard_map/ppermute | solution.py:39
  51.5 1.0 %shard_map.62.refs_4_ = bf16[3,1024,128]{2,1,0:T(8,128)(2,1)S(1)} custom-call(bf16[1024,128]{1,0:T(8,128)(2,1)S(1)} %copy-done.2, bf16[1024,128]{1,0:T(8,128)(2,1)} %collective-permute-done.1.refs_1_, bf16[1024,128]{1,0:T(8,128)(2,1)S(1)} %collective-permute-done.11.refs_2_), custom_call_target="tpu_custom_call" | custom-call | flops 1000 | bytes 1000 | tf_op jit(solution)/shard_map/pallas_call | solution.py:85
  52.5 1.1 %collective-permute-start.22 = (bf16[3,1024,128]{2,1,0:T(8,128)(2,1)S(1)}, bf16[3,1024,128]{2,1,0:T(8,128)(2,1)S(1)}, u32[]{:S(2)}, u32[]{:S(2)}) collective-permute-start(bf16[3,1024,128]{2,1,0:T(8,128)(2,1)S(1)} %shard_map.62.refs_4_), channel_id=1, source_target_pairs={{0,2},{1,3},{2,0},{3,1},{4,6},{5,7},{6,4},{7,5},{8,10},{9,11},{10,... | collective-permute-start | bytes 2359304 | tf_op jit(solution)/shard_map/ppermute | solution.py:45
  53.6 3.3 %shard_map.58 = (f32[3,256,768]{2,1,0:T(8,128)S(1)}, bf16[3,512,768]{2,1,0:T(8,128)(2,1)S(1)}) custom-call(bf16[256,768]{1,0:T(8,128)(2,1)} %bitcast.refs_0_, bf16[256,768]{1,0:T(8,128)(2,1)} %collective-permute-done.2.refs_1_, bf16[256,768]{1,0:T(8,128)(2,1)S(1)} %collective-permute-done.3.refs_2_, bf16[256,768]{1,0:T(8,128)(2,1)S(1)} %collective-permute-done.6.refs_3_, ...), custom_call_target="tpu_custom_call" | custom-call | flops 1000 | bytes 10501000 | tf_op jit(solution)/shard_map/pallas_call | solution.py:85
  57.0 0.0 copy-start.3
  57.0 1.7 %shard_map.59 = (bf16[4,256,256]{2,1,0:T(8,128)(2,1)S(1)}, bf16[4,16,128]{2,1,0:T(8,128)(2,1)S(1)}, bf16[2,256,512]{2,1,0:T(8,128)(2,1)S(1)}, bf16[2,256,512]{2,...) custom-call(bf16[256,768]{1,0:T(8,128)(2,1)S(1)} %collective-permute-done.4.refs_0_, ...), custom_call_target="tpu_custom_call" | custom-call | flops 1000 | bytes 17501000 | tf_op jit(solution)/shard_map/pallas_call | solution.py:85
  58.7 0.1 collective-permute-start.14
  58.8 0.5 collective-permute-start.15
  59.3 0.7 collective-permute-start.16
  59.9 0.7 collective-permute-start.17
  60.6 0.0 collective-permute-done.14.other.refs_7_
  60.7 1.0 %collective-permute-start.23 = (bf16[1024,128]{1,0:T(8,128)(2,1)S(1)}, bf16[1024,128]{1,0:T(8,128)(2,1)S(1)}, u32[]{:S(2)}, u32[]{:S(2)}) collective-permute-start(bf16[1024,128]{1,0:T(8,128)(2,1)S(1)} %collective-permute-done.13), channel_id=1, source_target_pairs={{0,2},{1,3},{2,0},{3,1},{4,6},{5,7},{6,4},{7,5},{8,10},{9,11},{10,... | collective-permute-start | bytes 786440 | tf_op jit(solution)/shard_map/ppermute | solution.py:45
  61.7 2.6 %shard_map.60 = (bf16[256,256]{1,0:T(8,128)(2,1)S(1)}, bf16[256,256]{1,0:T(8,128)(2,1)S(1)}) custom-call(s32[32]{0:T(128)S(1)} %copy-done.3, bf16[4,256,256]{2,1,0:T(8,128)(2,1)S(1)} %get-tuple-element.42.q.refs_3_, bf16[4,16,128]{2,1,0:T(8,128)(2,1)S(1)} %get-tuple-element.43.marks.refs_4_, bf16[2,256,512]{2,1,0:T(8,128)(2,1)S(1)} %get-tuple-element.47.kv.refs_5_, ...), custom_call_target="tpu_custom_call" | custom-call | flops 1000 | bytes 14001000 | tf_op jit(solution)/shard_map/pallas_call | solution.py:85
  64.3 2.7 %shard_map.61 = (bf16[256,256]{1,0:T(8,128)(2,1)S(1)}, bf16[256,256]{1,0:T(8,128)(2,1)S(1)}, bf16[256,256]{1,0:T(8,128)(2,1)S(1)}, bf16[256,256]{1,0:T(8,128)(2,1)S(1)}) custom-call(bf16[256,256]{1,0:T(8,128)(2,1)S(1)} %get-tuple-element.49.refs_0_, bf16[256,256]{1,0:T(8,128)(2,1)S(1)} %get-tuple-element.50.refs_1_, s32[32]{0:T(128)S(1)} %copy-done.3, ...), custom_call_target="tpu_custom_call" | custom-call | flops 1000 | bytes 14001000 | tf_op jit(solution)/shard_map/pallas_call | solution.py:85
  67.0 1.1 %collective-permute-start.18 = (bf16[256,256]{1,0:T(8,128)(2,1)S(1)}, bf16[256,256]{1,0:T(8,128)(2,1)S(1)}, u32[]{:S(2)}, u32[]{:S(2)}) collective-permute-start(bf16[256,256]{1,0:T(8,128)(2,1)S(1)} %get-tuple-element.54), channel_id=1, source_target_pairs={{0,2},{1,3},{2,0},{3,1},{4,6},{5,7},{6,4},{7,5},{8,10},{9,11},{10,... | collective-permute-start | bytes 393224 | tf_op jit(solution)/shard_map/ppermute | solution.py:45
  68.1 1.5 %collective-permute-start.19 = (bf16[256,256]{1,0:T(8,128)(2,1)S(1)}, bf16[256,256]{1,0:T(8,128)(2,1)S(1)}, u32[]{:S(2)}, u32[]{:S(2)}) collective-permute-start(bf16[256,256]{1,0:T(8,128)(2,1)S(1)} %get-tuple-element.55), channel_id=1, source_target_pairs={{0,16},{1,17},{2,18},{3,19},{4,20},{5,21},{6,22},{7,23},{8,24},{9,... | collective-permute-start | bytes 393224 | tf_op jit(solution)/shard_map/ppermute | solution.py:51
  69.6 1.0 %collective-permute-start.20 = (bf16[256,256]{1,0:T(8,128)(2,1)S(1)}, bf16[256,256]{1,0:T(8,128)(2,1)S(1)}, u32[]{:S(2)}, u32[]{:S(2)}) collective-permute-start(bf16[256,256]{1,0:T(8,128)(2,1)S(1)} %get-tuple-element.56), channel_id=1, source_target_pairs={{0,18},{1,19},{2,16},{3,17},{4,22},{5,23},{6,20},{7,21},{8,26},{9,... | collective-permute-start | bytes 393224 | tf_op jit(solution)/shard_map/ppermute | solution.py:51
  70.5 2.4 %collective-permute-done.22.refs_6_ = bf16[3,1024,128]{2,1,0:T(8,128)(2,1)S(1)} collective-permute-done((bf16[3,1024,128]{2,1,0:T(8,128)(2,1)S(1)}, bf16[3,1024,128]{2,1,0:T(8,128)(2,1)S(1)}, u32[]{:S(2)}, u32[]{:S(2)}) %collective-permute-start.22) | collective-permute-done | bytes 786464 | tf_op jit(solution)/shard_map/ppermute | solution.py:45
  72.9 3.0 %collective-permute-start.21 = (bf16[3,1024,128]{2,1,0:T(8,128)(2,1)S(1)}, bf16[3,1024,128]{2,1,0:T(8,128)(2,1)S(1)}, u32[]{:S(2)}, u32[]{:S(2)}) collective-permute-start(bf16[3,1024,128]{2,1,0:T(8,128)(2,1)S(1)} %shard_map.62.refs_4_), channel_id=1, source_target_pairs={{0,1},{1,0},{2,3},{3,2},{4,5},{5,4},{6,7},{7,6},{8,9},{9,8},{10,11... | collective-permute-start | bytes 2359304 | tf_op jit(solution)/shard_map/ppermute | solution.py:45
  76.0 7.5 %collective-permute-done.18.refs_1_ = bf16[256,256]{1,0:T(8,128)(2,1)S(1)} collective-permute-done((bf16[256,256]{1,0:T(8,128)(2,1)S(1)}, bf16[256,256]{1,0:T(8,128)(2,1)S(1)}, u32[]{:S(2)}, u32[]{:S(2)}) %collective-permute-start.18) | collective-permute-done | bytes 131104 | tf_op jit(solution)/shard_map/ppermute | solution.py:45
  83.5 0.1 collective-permute-start.24
  83.6 0.5 collective-permute-start.25
  84.1 0.1 collective-permute-start.26
  84.1 2.1 %collective-permute-done.25 = bf16[1024,128]{1,0:T(8,128)(2,1)S(1)} collective-permute-done((bf16[1024,128]{1,0:T(8,128)(2,1)S(1)}, bf16[1024,128]{1,0:T(8,128)(2,1)S(1)}, u32[]{:S(2)}, u32[]{:S(2)}) %collective-permute-start.25) | collective-permute-done | bytes 262176 | tf_op jit(solution)/shard_map/ppermute | solution.py:45
  86.2 0.4 collective-permute-done.26
  86.6 2.1 %shard_map.63 = bf16[256,2048]{1,0:T(8,128)(2,1)} custom-call(bf16[256,256]{1,0:T(8,128)(2,1)S(1)} %get-tuple-element.53.refs_0_, bf16[256,256]{1,0:T(8,128)(2,1)S(1)} %collective-permute-done.18.refs_1_, bf16[256,256]{1,0:T(8,128)(2,1)S(1)} %collective-permute-done.19.refs_2_, bf16[256,256]{1,0:T(8,128)(2,1)S(1)} %collective-permute-done.20.refs_3_, ...), custom_call_target="tpu_custom_call" | custom-call | flops 1000 | bytes 3501000 | tf_op jit(solution)/shard_map/pallas_call | solution.py:85
  (26 shorter events, 0.1 us)
Async XLA Ops:
  0.0 1.1 %copy-start.1 = (bf16[128,3072]{1,0:T(8,128)(2,1)S(1)}, bf16[128,3072]{1,0:T(8,128)(2,1)}, u32[]{:S(2)}) copy-start(bf16[128,3072]{1,0:T(8,128)(2,1)} %w.1) | copy-start | bytes 2359300
  1.3 11.2 %collective-permute-start.1 = (bf16[1024,128]{1,0:T(8,128)(2,1)}, bf16[1024,128]{1,0:T(8,128)(2,1)}, u32[]{:S(2)}, u32[]{:S(2)}) collective-permute-start(bf16[1024,128]{1,0:T(8,128)(2,1)} %refs_0_), channel_id=1, source_target_pairs={{0,8},{1,9},{2,10},{3,11},{8,12},{9,13},{10,14},{11,15},{12,4},{13... | collective-permute-start | bytes 786440 | tf_op jit(solution)/shard_map/ppermute | solution.py:39
  5.4 6.4 %collective-permute-start = (bf16[128,768]{1,0:T(8,128)(2,1)S(1)}, bf16[128,768]{1,0:T(8,128)(2,1)S(1)}, u32[]{:S(2)}, u32[]{:S(2)}) collective-permute-start(bf16[128,768]{1,0:T(8,128)(2,1)S(1)} %get-tuple-element.34), channel_id=1, source_target_pairs={{0,2},{1,3},{2,0},{3,1},{4,6},{5,7},{6,4},{7,5},{8,10},{9,11},{10,... | collective-permute-start | bytes 589832 | tf_op jit(solution)/shard_map/ppermute | solution.py:45
  6.9 1.2 %copy-start = (bf16[256,2048]{1,0:T(8,128)(2,1)S(1)}, bf16[256,2048]{1,0:T(8,128)(2,1)}, u32[]{:S(2)}) copy-start(bf16[256,2048]{1,0:T(8,128)(2,1)} %x) | copy-start | bytes 3145732
  8.1 0.7 copy-start.4
  9.4 25.8 %collective-permute-start.10 = (bf16[272,2048]{1,0:T(8,128)(2,1)S(1)}, bf16[272,2048]{1,0:T(8,128)(2,1)S(1)}, u32[]{:S(2)}, u32[]{:S(2)}) collective-permute-start(bf16[272,2048]{1,0:T(8,128)(2,1)S(1)} %shard_map.57.refs_6_.refs_4_), channel_id=1, source_target_pairs={{0,16},{1,17},{2,18},{3,19},{4,20},{5,21},{6,22},{7,23},{8,24},{9,... | collective-permute-start | bytes 3342344 | tf_op jit(solution)/shard_map/ppermute | solution.py:51
  12.5 25.2 %collective-permute-start.9 = (bf16[272,2048]{1,0:T(8,128)(2,1)S(1)}, bf16[272,2048]{1,0:T(8,128)(2,1)S(1)}, u32[]{:S(2)}, u32[]{:S(2)}) collective-permute-start(bf16[272,2048]{1,0:T(8,128)(2,1)S(1)} %shard_map.57.refs_6_.refs_4_), channel_id=1, source_target_pairs={{0,2},{1,3},{2,0},{3,1},{4,6},{5,7},{6,4},{7,5},{8,10},{9,11},{10,... | collective-permute-start | bytes 3342344 | tf_op jit(solution)/shard_map/ppermute | solution.py:45
  14.0 12.4 %collective-permute-start.2 = (bf16[256,768]{1,0:T(8,128)(2,1)}, bf16[256,768]{1,0:T(8,128)(2,1)}, u32[]{:S(2)}, u32[]{:S(2)}) collective-permute-start(bf16[256,768]{1,0:T(8,128)(2,1)} %bitcast.refs_0_), channel_id=1, source_target_pairs={{0,8},{1,9},{2,10},{3,11},{8,12},{9,13},{10,14},{11,15},{12,4},{13... | collective-permute-start | bytes 1179656 | tf_op jit(solution)/shard_map/ppermute | solution.py:39
  16.1 35.3 %copy-start.2 = (bf16[1024,128]{1,0:T(8,128)(2,1)S(1)}, bf16[1024,128]{1,0:T(8,128)(2,1)}, u32[]{:S(2)}) copy-start(bf16[1024,128]{1,0:T(8,128)(2,1)} %refs_0_) | copy-start | bytes 786436
  16.1 21.7 %collective-permute-start.6 = (bf16[256,768]{1,0:T(8,128)(2,1)}, bf16[256,768]{1,0:T(8,128)(2,1)S(1)}, u32[]{:S(2)}, u32[]{:S(2)}) collective-permute-start(bf16[256,768]{1,0:T(8,128)(2,1)} %bitcast.refs_0_), channel_id=1, source_target_pairs={{0,1},{1,0},{2,3},{3,2},{4,5},{5,4},{6,7},{7,6},{8,9},{9,8},{10,11... | collective-permute-start | bytes 1179656 | tf_op jit(solution)/shard_map/ppermute | solution.py:45
  16.1 21.7 %collective-permute-start.11 = (bf16[1024,128]{1,0:T(8,128)(2,1)}, bf16[1024,128]{1,0:T(8,128)(2,1)S(1)}, u32[]{:S(2)}, u32[]{:S(2)}) collective-permute-start(bf16[1024,128]{1,0:T(8,128)(2,1)} %collective-permute-done.1.refs_1_), channel_id=1, source_target_pairs={{0,8},{1,9},{2,10},{3,11},{8,12},{9,13},{10,14},{11,15},{12,4},{13... | collective-permute-start | bytes 786440 | tf_op jit(solution)/shard_map/ppermute | solution.py:39
  26.4 11.5 %collective-permute-start.3 = (bf16[256,768]{1,0:T(8,128)(2,1)}, bf16[256,768]{1,0:T(8,128)(2,1)S(1)}, u32[]{:S(2)}, u32[]{:S(2)}) collective-permute-start(bf16[256,768]{1,0:T(8,128)(2,1)} %collective-permute-done.2.refs_1_), channel_id=1, source_target_pairs={{0,8},{1,9},{2,10},{3,11},{8,12},{9,13},{10,14},{11,15},{12,4},{13... | collective-permute-start | bytes 1179656 | tf_op jit(solution)/shard_map/ppermute | solution.py:39
  35.2 2.7 %collective-permute-start.7 = (bf16[256,768]{1,0:T(8,128)(2,1)}, bf16[256,768]{1,0:T(8,128)(2,1)S(1)}, u32[]{:S(2)}, u32[]{:S(2)}) collective-permute-start(bf16[256,768]{1,0:T(8,128)(2,1)} %collective-permute-done.2.refs_1_), channel_id=1, source_target_pairs={{0,1},{1,0},{2,3},{3,2},{4,5},{5,4},{6,7},{7,6},{8,9},{9,8},{10,11... | collective-permute-start | bytes 1179656 | tf_op jit(solution)/shard_map/ppermute | solution.py:45
  37.9 19.1 %collective-permute-start.12 = (bf16[272,2048]{1,0:T(8,128)(2,1)S(1)}, bf16[272,2048]{1,0:T(8,128)(2,1)S(1)}, u32[]{:S(2)}, u32[]{:S(2)}) collective-permute-start(bf16[272,2048]{1,0:T(8,128)(2,1)S(1)} %broadcast_select_fusion), channel_id=1, source_target_pairs={{0,16},{1,3},{2,18},{3,1},{4,20},{5,7},{6,22},{7,5},{8,24},{9,11},... | collective-permute-start | bytes 3342344 | tf_op jit(solution)/shard_map/ppermute | solution.py:61
  39.4 9.1 %collective-permute-start.4 = (bf16[256,768]{1,0:T(8,128)(2,1)S(1)}, bf16[256,768]{1,0:T(8,128)(2,1)S(1)}, u32[]{:S(2)}, u32[]{:S(2)}) collective-permute-start(bf16[256,768]{1,0:T(8,128)(2,1)S(1)} %collective-permute-done.3.refs_2_), channel_id=1, source_target_pairs={{0,8},{1,9},{2,10},{3,11},{8,12},{9,13},{10,14},{11,15},{12,4},{13... | collective-permute-start | bytes 1179656 | tf_op jit(solution)/shard_map/ppermute | solution.py:39
  42.5 11.1 %collective-permute-start.8 = (bf16[256,768]{1,0:T(8,128)(2,1)S(1)}, bf16[256,768]{1,0:T(8,128)(2,1)S(1)}, u32[]{:S(2)}, u32[]{:S(2)}) collective-permute-start(bf16[256,768]{1,0:T(8,128)(2,1)S(1)} %collective-permute-done.3.refs_2_), channel_id=1, source_target_pairs={{0,1},{1,0},{2,3},{3,2},{4,5},{5,4},{6,7},{7,6},{8,9},{9,8},{10,11... | collective-permute-start | bytes 1179656 | tf_op jit(solution)/shard_map/ppermute | solution.py:45
  48.5 8.4 %collective-permute-start.5 = (bf16[256,768]{1,0:T(8,128)(2,1)S(1)}, bf16[256,768]{1,0:T(8,128)(2,1)S(1)}, u32[]{:S(2)}, u32[]{:S(2)}) collective-permute-start(bf16[256,768]{1,0:T(8,128)(2,1)S(1)} %collective-permute-done.4.refs_0_), channel_id=1, source_target_pairs={{0,1},{1,0},{2,3},{3,2},{4,5},{5,4},{6,7},{7,6},{8,9},{9,8},{10,11... | collective-permute-start | bytes 1179656 | tf_op jit(solution)/shard_map/ppermute | solution.py:45
  48.5 10.2 %collective-permute-start.13 = (bf16[1024,128]{1,0:T(8,128)(2,1)S(1)}, bf16[1024,128]{1,0:T(8,128)(2,1)S(1)}, u32[]{:S(2)}, u32[]{:S(2)}) collective-permute-start(bf16[1024,128]{1,0:T(8,128)(2,1)S(1)} %collective-permute-done.11.refs_2_), channel_id=1, source_target_pairs={{0,8},{1,9},{2,10},{3,11},{8,12},{9,13},{10,14},{11,15},{12,4},{13... | collective-permute-start | bytes 786440 | tf_op jit(solution)/shard_map/ppermute | solution.py:39
  52.5 20.4 %collective-permute-start.22 = (bf16[3,1024,128]{2,1,0:T(8,128)(2,1)S(1)}, bf16[3,1024,128]{2,1,0:T(8,128)(2,1)S(1)}, u32[]{:S(2)}, u32[]{:S(2)}) collective-permute-start(bf16[3,1024,128]{2,1,0:T(8,128)(2,1)S(1)} %shard_map.62.refs_4_), channel_id=1, source_target_pairs={{0,2},{1,3},{2,0},{3,1},{4,6},{5,7},{6,4},{7,5},{8,10},{9,11},{10,... | collective-permute-start | bytes 2359304 | tf_op jit(solution)/shard_map/ppermute | solution.py:45
  57.0 4.7 %copy-start.3 = (s32[32]{0:T(128)S(1)}, s32[32]{0:T(128)}, u32[]{:S(2)}) copy-start(s32[32]{0:T(128)} %refs_2_.1) | copy-start | bytes 388
  58.7 2.0 %collective-permute-start.14 = (bf16[2,256,512]{2,1,0:T(8,128)(2,1)S(1)}, bf16[2,256,512]{2,1,0:T(8,128)(2,1)S(1)}, u32[]{:S(2)}, u32[]{:S(2)}) collective-permute-start(bf16[2,256,512]{2,1,0:T(8,128)(2,1)S(1)} %get-tuple-element.47.kv.refs_5_), channel_id=1, source_target_pairs={{0,1},{1,0},{2,3},{3,2},{4,5},{5,4},{6,7},{7,6},{8,9},{9,8},{10,11... | collective-permute-start | bytes 1572872 | tf_op jit(solution)/shard_map/ppermute | solution.py:45
  58.8 2.9 %collective-permute-start.15 = (bf16[2,256,512]{2,1,0:T(8,128)(2,1)S(1)}, bf16[2,256,512]{2,1,0:T(8,128)(2,1)S(1)}, u32[]{:S(2)}, u32[]{:S(2)}) collective-permute-start(bf16[2,256,512]{2,1,0:T(8,128)(2,1)S(1)} %get-tuple-element.48.kv_across.refs_6_), channel_id=1, source_target_pairs={{0,1},{1,0},{2,3},{3,2},{4,5},{5,4},{6,7},{7,6},{8,9},{9,8},{10,11... | collective-permute-start | bytes 1572872 | tf_op jit(solution)/shard_map/ppermute | solution.py:45
  59.3 5.1 %collective-permute-start.16 = (bf16[256,512]{1,0:T(8,128)(2,1)S(1)}, bf16[256,512]{1,0:T(8,128)(2,1)S(1)}, u32[]{:S(2)}, u32[]{:S(2)}) collective-permute-start(bf16[256,512]{1,0:T(8,128)(2,1)S(1)} %get-tuple-element.51), channel_id=1, source_target_pairs={{1,4},{3,6},{4,1},{5,8},{6,3},{7,10},{8,5},{9,12},{10,7},{11,14},{... | collective-permute-start | bytes 786440 | tf_op jit(solution)/shard_map/ppermute | solution.py:67
  59.9 4.4 %collective-permute-start.17 = (bf16[256,512]{1,0:T(8,128)(2,1)S(1)}, bf16[256,512]{1,0:T(8,128)(2,1)S(1)}, u32[]{:S(2)}, u32[]{:S(2)}) collective-permute-start(bf16[256,512]{1,0:T(8,128)(2,1)S(1)} %get-tuple-element.52), channel_id=1, source_target_pairs={{1,4},{3,6},{4,1},{5,8},{6,3},{7,10},{8,5},{9,12},{10,7},{11,14},{... | collective-permute-start | bytes 786440 | tf_op jit(solution)/shard_map/ppermute | solution.py:67
  60.7 22.8 %collective-permute-start.23 = (bf16[1024,128]{1,0:T(8,128)(2,1)S(1)}, bf16[1024,128]{1,0:T(8,128)(2,1)S(1)}, u32[]{:S(2)}, u32[]{:S(2)}) collective-permute-start(bf16[1024,128]{1,0:T(8,128)(2,1)S(1)} %collective-permute-done.13), channel_id=1, source_target_pairs={{0,2},{1,3},{2,0},{3,1},{4,6},{5,7},{6,4},{7,5},{8,10},{9,11},{10,... | collective-permute-start | bytes 786440 | tf_op jit(solution)/shard_map/ppermute | solution.py:45
  67.0 16.5 %collective-permute-start.18 = (bf16[256,256]{1,0:T(8,128)(2,1)S(1)}, bf16[256,256]{1,0:T(8,128)(2,1)S(1)}, u32[]{:S(2)}, u32[]{:S(2)}) collective-permute-start(bf16[256,256]{1,0:T(8,128)(2,1)S(1)} %get-tuple-element.54), channel_id=1, source_target_pairs={{0,2},{1,3},{2,0},{3,1},{4,6},{5,7},{6,4},{7,5},{8,10},{9,11},{10,... | collective-permute-start | bytes 393224 | tf_op jit(solution)/shard_map/ppermute | solution.py:45
  68.1 15.4 %collective-permute-start.19 = (bf16[256,256]{1,0:T(8,128)(2,1)S(1)}, bf16[256,256]{1,0:T(8,128)(2,1)S(1)}, u32[]{:S(2)}, u32[]{:S(2)}) collective-permute-start(bf16[256,256]{1,0:T(8,128)(2,1)S(1)} %get-tuple-element.55), channel_id=1, source_target_pairs={{0,16},{1,17},{2,18},{3,19},{4,20},{5,21},{6,22},{7,23},{8,24},{9,... | collective-permute-start | bytes 393224 | tf_op jit(solution)/shard_map/ppermute | solution.py:51
  69.6 13.9 %collective-permute-start.20 = (bf16[256,256]{1,0:T(8,128)(2,1)S(1)}, bf16[256,256]{1,0:T(8,128)(2,1)S(1)}, u32[]{:S(2)}, u32[]{:S(2)}) collective-permute-start(bf16[256,256]{1,0:T(8,128)(2,1)S(1)} %get-tuple-element.56), channel_id=1, source_target_pairs={{0,18},{1,19},{2,16},{3,17},{4,22},{5,23},{6,20},{7,21},{8,26},{9,... | collective-permute-start | bytes 393224 | tf_op jit(solution)/shard_map/ppermute | solution.py:51
  72.9 13.6 %collective-permute-start.21 = (bf16[3,1024,128]{2,1,0:T(8,128)(2,1)S(1)}, bf16[3,1024,128]{2,1,0:T(8,128)(2,1)S(1)}, u32[]{:S(2)}, u32[]{:S(2)}) collective-permute-start(bf16[3,1024,128]{2,1,0:T(8,128)(2,1)S(1)} %shard_map.62.refs_4_), channel_id=1, source_target_pairs={{0,1},{1,0},{2,3},{3,2},{4,5},{5,4},{6,7},{7,6},{8,9},{9,8},{10,11... | collective-permute-start | bytes 2359304 | tf_op jit(solution)/shard_map/ppermute | solution.py:45
  83.5 3.1 %collective-permute-start.24 = (bf16[3,1024,128]{2,1,0:T(8,128)(2,1)S(1)}, bf16[3,1024,128]{2,1,0:T(8,128)(2,1)S(1)}, u32[]{:S(2)}, u32[]{:S(2)}) collective-permute-start(bf16[3,1024,128]{2,1,0:T(8,128)(2,1)S(1)} %collective-permute-done.22.refs_6_), channel_id=1, source_target_pairs={{0,1},{1,0},{2,3},{3,2},{4,5},{5,4},{6,7},{7,6},{8,9},{9,8},{10,11... | collective-permute-start | bytes 2359304 | tf_op jit(solution)/shard_map/ppermute | solution.py:45
  83.6 2.6 %collective-permute-start.25 = (bf16[1024,128]{1,0:T(8,128)(2,1)S(1)}, bf16[1024,128]{1,0:T(8,128)(2,1)S(1)}, u32[]{:S(2)}, u32[]{:S(2)}) collective-permute-start(bf16[1024,128]{1,0:T(8,128)(2,1)S(1)} %collective-permute-done.13), channel_id=1, source_target_pairs={{0,1},{1,0},{2,3},{3,2},{4,5},{5,4},{6,7},{7,6},{8,9},{9,8},{10,11... | collective-permute-start | bytes 786440 | tf_op jit(solution)/shard_map/ppermute | solution.py:45
  84.1 2.5 %collective-permute-start.26 = (bf16[1024,128]{1,0:T(8,128)(2,1)S(1)}, bf16[1024,128]{1,0:T(8,128)(2,1)S(1)}, u32[]{:S(2)}, u32[]{:S(2)}) collective-permute-start(bf16[1024,128]{1,0:T(8,128)(2,1)S(1)} %collective-permute-done.23), channel_id=1, source_target_pairs={{0,1},{1,0},{2,3},{3,2},{4,5},{5,4},{6,7},{7,6},{8,9},{9,8},{10,11... | collective-permute-start | bytes 786440 | tf_op jit(solution)/shard_map/ppermute | solution.py:45

commit v3 on v2

--- a/solution.py
+++ b/solution.py
@@ -30,13 +30,18 @@
     return jnp.where(2 * at < count, 2 * at, 2 * (count - at) - 1)
 
 
-def along_ring(x):
-    count = lax.axis_size("inner") // 4
+def along_ring(x, both_ways=False):
+    outer, inner = lax.axis_size("outer"), lax.axis_size("inner")
+    count = inner // 4
     order = [z for z in range(0, count, 2)] + [z for z in range(count - 1, 0, -1) if z % 2]
-    pairs = [
-        (4 * z + j, 4 * order[(n + 1) % count] + j) for n, z in enumerate(order) for j in range(4)
-    ]
-    return lax.ppermute(x, "inner", pairs)
+    pairs = []
+    for o in range(outer):
+        for n in range(count):
+            source, target = order[n], order[(n + 1) % count]
+            if both_ways and o % 2:
+                source, target = target, source
+            pairs += [(o * inner + 4 * source + j, o * inner + 4 * target + j) for j in range(4)]
+    return lax.ppermute(x, ("outer", "inner"), pairs)
 
 
 def swap(x, r):
@@ -246,7 +251,7 @@
 
 
 def finish_body(count, *refs):
-    contexts, refs = refs[:4], refs[4:]
+    contexts, refs = refs[3::-1], refs[4:]
     out, context, tiles, sems = refs[-4:]
     bundles = refs[:-4]
     side, y, core = place()
@@ -255,20 +260,22 @@
         pair = 2 * lax.rem(side + b // 2, 2) + lax.rem(y + b % 2, 2)
         context[pair] = piece[...]
     whole = jnp.concatenate([context[pair] for pair in range(4)], axis=1)
-    for step in range(count):
-        at, n = (4, 0) if step == count - 1 else (0, step)
-        for which_y, k in ((y, 0), (1 - y, 2)):
-            mine, other = bundles[at + k][n], bundles[at + k + 1][n]
-            tile = jnp.concatenate(
-                [jnp.where(core == 0, mine, other), jnp.where(core == 0, other, mine)], axis=1
-            )
-            column = pl.multiple_of((4 * ring_source(step, count) + 2 * which_y) * HD, HD)
-            done = jnp.dot(whole, tile, preferred_element_type=F32)
-            m = len(copies)
-            tiles[m] = done.astype(BF16)
-            into = out.at[:, pl.ds(column, PAIR)]
-            copies.append(pltpu.make_async_copy(tiles.at[m], into, sems.at[m]))
-            copies[-1].start()
+    here, here_next, others, others_next, there, there_next, late, late_next = bundles
+    strips = [(n, y, here[n], here_next[n]) for n in range(3)]
+    strips += [(2 * n, 1 - y, others[n], others_next[n]) for n in range(2)]
+    strips += [(1, 1 - y, there[0], there_next[0])]
+    strips += [(3, y, late[0], late_next[0]), (3, 1 - y, late[1], late_next[1])]
+    for step, which_y, mine, other in strips:
+        tile = jnp.concatenate(
+            [jnp.where(core == 0, mine, other), jnp.where(core == 0, other, mine)], axis=1
+        )
+        z = ring_source(step + side * (count - 2 * step), count)
+        column = pl.multiple_of((4 * z + 2 * which_y) * HD, HD)
+        m = len(copies)
+        tiles[m] = jnp.dot(whole, tile, preferred_element_type=F32).astype(BF16)
+        into = out.at[:, pl.ds(column, PAIR)]
+        copies.append(pltpu.make_async_copy(tiles.at[m], into, sems.at[m]))
+        copies[-1].start()
     for copy in copies:
         copy.wait()
 
@@ -295,22 +302,22 @@
     got = swap(send, 2)
     strips = [w_out]
     if count > 1:
-        strips.append(along_ring(after(w_out, send)))
+        strips.append(along_ring(after(w_out, send), True))
     piece = stack([mine, got], cost=1.0).reshape(2 * w_rows, wide)
     block_y = swap(after(normed, piece, *strips[1:]), 2)
     pieces = [after(piece, *strips[1:])]
     for _ in range(count - 1):
         pieces.append(along_ring(pieces[-1]))
-    next_pieces = [swap(p, 1) for p in pieces]
+    next_pieces = [swap(p, 1) for p in pieces[:-2]]
     block_d = jnp.where(core == 0, block_y, block_x)
     for n in range(1, count - 2):
-        strips.append(along_ring(strips[-1]))
+        strips.append(along_ring(strips[-1], True))
+    here = stack(strips)
+    next_pieces += [swap(after(pieces[-2], here), 1), swap(pieces[-1], 1)]
     block_d = after(block_d, *strips[1:], *pieces[: count - 1], *next_pieces[: count - 2])
     block_d = swap_by_core(block_d, 4, 2)
-    for n in range(len(strips), count):
-        strips.append(along_ring(after(strips[-1], pieces[-1])))
-    here = stack([after(strips[0], pieces[-1])] + strips[1:-1])
-    there = swap(here, 2)
+    there = swap(after(strips[1], pieces[-1]), 2)
+    there_across = swap(there, 4)
     total, weights = call(
         functools.partial(project_body, count),
         [((3, rows, wide), F32), (count - 1, 4 * w_rows, wide)],
@@ -325,10 +332,11 @@
         cost=5.0,
     )
     halo, halo_across = to_next_group(halo), to_next_group(halo_across)
-    next_kv = [swap(after(b, strips[-1]), 1) for b in kv]
-    here_last = after(strips[-1], next_kv[0])
-    there_last = swap(here_last, 2)
-    here_next, here_last_next = swap(after(here, next_kv[0]), 1), swap(here_last, 1)
+    next_kv = [swap(b, 1) for b in kv]
+    there_next = swap(there, 1)
+    others = stack([after(strips[0], pieces[-1]), strips[2]])
+    others = swap(others, 2)
+    here_next = swap(after(here, next_kv[0]), 1)
     beyond = []
     if wider:
         upper = [jnp.where(side == 1, kv[0][b], kv[1][b]) for b in range(2)]
@@ -340,10 +348,11 @@
     inside = call(
         functools.partial(attend_body, 0, wider),
         [context] * 2,
-        held + beyond,
+        [after(counts, there_next)] + held[1:] + beyond,
         specs=[SMEM] + [VMEM] * (len(held + beyond) - 1),
         cost=4.0,
     )
+    here_last = along_ring(after(strips[-1], inside[0]), True)
     held = list(inside) + held + [halo, halo_across] + beyond
     c_0, c_1, c_2, c_3 = call(
         functools.partial(attend_edge_body, wider),
@@ -354,14 +363,14 @@
         cost=4.0,
     )
     contexts = [c_0, swap(c_1, 2), swap(c_2, 4), swap(c_3, 6)]
-    there_next = swap(after(there, there_last, *contexts[1:]), 1)
-    there_last_next = swap(there_last, 1)
-    bundles = [here, here_next, there, there_next]
-    bundles += [b[None] for b in (here_last, here_last_next, there_last, there_last_next)]
+    others_next = swap(after(others, c_3), 1)
+    late = stack([here_last, there_across])
+    late_next = swap(after(late, *contexts[1:]), 1)
+    bundles = [here, here_next, others, others_next, there[None], there_next[None], late, late_next]
     return call(
         functools.partial(finish_body, count),
         (rows, width),
-        contexts + bundles,
+        contexts[::-1] + bundles,
         out_spec=ANY,
         scratch=[
             pltpu.VMEM((4, rows, PAIR), BF16),

time: 88.9 us -> 87.5 us (0.984)
  waiting for transfers between devices: 37.1 us -> 35.2 us
    ppermute x15, waiting for transfers between devices: 15.7 us -> 8.87 us  [swap(): return lax.ppermute(x, 'inner', [(i, i ^ r) for i in range(inner)])]
    ppermute x3 -> x4, waiting for transfers between devices: 5.79 us -> 10.3 us  [swap(): return lax.ppermute(x, ('outer', 'inner'), pairs)]
    ppermute x6, starting transfers between devices: 15.9 us -> 18.5 us  [along_ring(): return lax.ppermute(x, ('outer', 'inner'), pairs)]
    ppermute x15, starting transfers between devices: 10.5 us -> 8.31 us  [swap(): return lax.ppermute(x, 'inner', [(i, i ^ r) for i in range(inner)])]
    pallas_call x9 -> x11, Pallas kernels: 14.9 us -> 15 us  [call(): pl.pallas_call(body, out_shape=outs if many else outs[0], in_specs=specs...]
    ppermute x3 -> x4, starting transfers between devices: 4.02 us -> 4 us  [swap(): return lax.ppermute(x, ('outer', 'inner'), pairs)]
  transfers between devices with their start and end apart: 27 -> 28, of which waited for: 9 -> 11; matrix products, arithmetic and copies ran while one was open for 0% -> 0% of each run, Pallas kernels for 14% -> 15%
where the time goes in v3:
time: 87.5 us; the launch traced here: 87.3 us
  waiting for transfers between devices  35.2 us (40%)
  starting transfers between devices  33.8 us (39%)
  Pallas kernels  15 us (17%)
  local copies, waits for them, and re-layouts  3.02 us (3%)
    ppermute x6, starting transfers between devices, along_ring(): return lax.ppermute(x, ('outer', 'inner'), pairs)  18.5 us
    ppermute x6, waiting for transfers between devices, along_ring(): return lax.ppermute(x, ('outer', 'inner'), pairs)  16 us
    pallas_call x11, Pallas kernels, call(): pl.pallas_call(body, out_shape=outs if many else outs[0], in_specs=specs...  15 us
    ppermute x4, waiting for transfers between devices, swap(): return lax.ppermute(x, ('outer', 'inner'), pairs)  10.3 us
    ppermute x15, waiting for transfers between devices, swap(): return lax.ppermute(x, 'inner', [(i, i ^ r) for i in range(inner)])  8.87 us
    ppermute x15, starting transfers between devices, swap(): return lax.ppermute(x, 'inner', [(i, i ^ r) for i in range(inner)])  8.31 us
    ppermute x4, starting transfers between devices, swap(): return lax.ppermute(x, ('outer', 'inner'), pairs)  4 us
    unnamed x10, local copies, waits for them, and re-layouts  3.02 us
  transfers between devices with their start and end apart: 28, of which 11 were waited for; matrix products, arithmetic and copies ran while one was open for 0% of the time, Pallas kernels for 15%

profile of v3, /device:TPU:0, one launch (start us, length us, event | category | flops | bytes accessed | tf_op | source)
XLA Modules:
  0.0 87.3 jit_solution(15027603987493100311)
XLA Ops:
  0.0 1.1 %copy-done.2 = bf16[128,3072]{1,0:T(8,128)(2,1)S(1)} copy-done((bf16[128,3072]{1,0:T(8,128)(2,1)S(1)}, bf16[128,3072]{1,0:T(8,128)(2,1)}, u32[]{:S(2)}) %copy-start.2) | copy-done | bytes 786456
  1.1 0.1 shard_map.55
  1.3 4.1 %collective-permute-start = (bf16[1024,128]{1,0:T(8,128)(2,1)}, bf16[1024,128]{1,0:T(8,128)(2,1)}, u32[]{:S(2)}, u32[]{:S(2)}) collective-permute-start(bf16[1024,128]{1,0:T(8,128)(2,1)} %refs_0_.2), channel_id=1, source_target_pairs={{0,8},{1,9},{2,10},{3,11},{8,12},{9,13},{10,14},{11,15},{12,4},{13... | collective-permute-start | bytes 786440 | tf_op jit(solution)/shard_map/ppermute | solution.py:44
  5.4 1.5 %collective-permute-start.1 = (bf16[128,768]{1,0:T(8,128)(2,1)S(1)}, bf16[128,768]{1,0:T(8,128)(2,1)S(1)}, u32[]{:S(2)}, u32[]{:S(2)}) collective-permute-start(bf16[128,768]{1,0:T(8,128)(2,1)S(1)} %get-tuple-element.34), channel_id=1, source_target_pairs={{0,2},{1,3},{2,0},{3,1},{4,6},{5,7},{6,4},{7,5},{8,10},{9,11},{10,... | collective-permute-start | bytes 589832 | tf_op jit(solution)/shard_map/ppermute | solution.py:50
  6.9 1.2 %copy-done = bf16[256,2048]{1,0:T(8,128)(2,1)S(1)} copy-done((bf16[256,2048]{1,0:T(8,128)(2,1)S(1)}, bf16[256,2048]{1,0:T(8,128)(2,1)}, u32[]{:S(2)}) %copy-start) | copy-done | bytes 1048600
  8.1 0.7 copy-done.4
  8.8 0.6 shard_map.58.refs_6_.refs_4_
  9.4 0.5 collective-permute-start.13
  9.9 1.8 %collective-permute-done.1.refs_1_ = bf16[128,768]{1,0:T(8,128)(2,1)S(1)} collective-permute-done((bf16[128,768]{1,0:T(8,128)(2,1)S(1)}, bf16[128,768]{1,0:T(8,128)(2,1)S(1)}, u32[]{:S(2)}, u32[]{:S(2)}) %collective-permute-start.1) | collective-permute-done | bytes 196640 | tf_op jit(solution)/shard_map/ppermute | solution.py:50
  11.7 0.8 shard_map.56
  12.5 0.0 collective-permute-done.refs_1_
  12.5 1.5 %collective-permute-start.12 = (bf16[272,2048]{1,0:T(8,128)(2,1)S(1)}, bf16[272,2048]{1,0:T(8,128)(2,1)S(1)}, u32[]{:S(2)}, u32[]{:S(2)}) collective-permute-start(bf16[272,2048]{1,0:T(8,128)(2,1)S(1)} %shard_map.58.refs_6_.refs_4_), channel_id=1, source_target_pairs={{0,2},{1,3},{2,0},{3,1},{4,6},{5,7},{6,4},{7,5},{8,10},{9,11},{10,... | collective-permute-start | bytes 3342344 | tf_op jit(solution)/shard_map/ppermute | solution.py:50
  14.0 2.1 %collective-permute-start.2 = (bf16[256,768]{1,0:T(8,128)(2,1)}, bf16[256,768]{1,0:T(8,128)(2,1)}, u32[]{:S(2)}, u32[]{:S(2)}) collective-permute-start(bf16[256,768]{1,0:T(8,128)(2,1)} %bitcast.refs_0_), channel_id=1, source_target_pairs={{0,8},{1,9},{2,10},{3,11},{8,12},{9,13},{10,14},{11,15},{12,4},{13... | collective-permute-start | bytes 1179656 | tf_op jit(solution)/shard_map/ppermute | solution.py:44
  16.1 0.7 collective-permute-start.10
  16.8 9.6 %collective-permute-done.2.refs_1_ = bf16[256,768]{1,0:T(8,128)(2,1)} collective-permute-done((bf16[256,768]{1,0:T(8,128)(2,1)}, bf16[256,768]{1,0:T(8,128)(2,1)}, u32[]{:S(2)}, u32[]{:S(2)}) %collective-permute-start.2) | collective-permute-done | bytes 393248 | tf_op jit(solution)/shard_map/ppermute | solution.py:44
  26.4 3.0 %collective-permute-start.3 = (bf16[256,768]{1,0:T(8,128)(2,1)}, bf16[256,768]{1,0:T(8,128)(2,1)S(1)}, u32[]{:S(2)}, u32[]{:S(2)}) collective-permute-start(bf16[256,768]{1,0:T(8,128)(2,1)} %collective-permute-done.2.refs_1_), channel_id=1, source_target_pairs={{0,8},{1,9},{2,10},{3,11},{8,12},{9,13},{10,14},{11,15},{12,4},{13... | collective-permute-start | bytes 1179656 | tf_op jit(solution)/shard_map/ppermute | solution.py:44
  29.4 5.8 %collective-permute-done.13.refs_8_.refs_6_ = bf16[272,2048]{1,0:T(8,128)(2,1)S(1)} collective-permute-done((bf16[272,2048]{1,0:T(8,128)(2,1)S(1)}, bf16[272,2048]{1,0:T(8,128)(2,1)S(1)}, u32[]{:S(2)}, u32[]{:S(2)}) %collective-permute-start.13) | collective-permute-done | bytes 1114144 | tf_op jit(solution)/shard_map/ppermute | solution.py:56
  35.2 2.5 %collective-permute-done.12.refs_7_.refs_5_ = bf16[272,2048]{1,0:T(8,128)(2,1)S(1)} collective-permute-done((bf16[272,2048]{1,0:T(8,128)(2,1)S(1)}, bf16[272,2048]{1,0:T(8,128)(2,1)S(1)}, u32[]{:S(2)}, u32[]{:S(2)}) %collective-permute-start.12) | collective-permute-done | bytes 1114144 | tf_op jit(solution)/shard_map/ppermute | solution.py:50
  37.7 0.1 broadcast_select_fusion
  37.9 1.6 %collective-permute-start.14 = (bf16[272,2048]{1,0:T(8,128)(2,1)S(1)}, bf16[272,2048]{1,0:T(8,128)(2,1)S(1)}, u32[]{:S(2)}, u32[]{:S(2)}) collective-permute-start(bf16[272,2048]{1,0:T(8,128)(2,1)S(1)} %broadcast_select_fusion), channel_id=1, source_target_pairs={{0,16},{1,3},{2,18},{3,1},{4,20},{5,7},{6,22},{7,5},{8,24},{9,11},... | collective-permute-start | bytes 3342344 | tf_op jit(solution)/shard_map/ppermute | solution.py:66
  39.5 2.1 %collective-permute-start.4 = (bf16[256,768]{1,0:T(8,128)(2,1)S(1)}, bf16[256,768]{1,0:T(8,128)(2,1)S(1)}, u32[]{:S(2)}, u32[]{:S(2)}) collective-permute-start(bf16[256,768]{1,0:T(8,128)(2,1)S(1)} %collective-permute-done.3.refs_2_), channel_id=1, source_target_pairs={{0,8},{1,9},{2,10},{3,11},{8,12},{9,13},{10,14},{11,15},{12,4},{13... | collective-permute-start | bytes 1179656 | tf_op jit(solution)/shard_map/ppermute | solution.py:44
  41.6 1.0 %shard_map.57.refs_4_ = bf16[3,1024,128]{2,1,0:T(8,128)(2,1)S(1)} custom-call(bf16[1024,128]{1,0:T(8,128)(2,1)S(1)} %copy-done.1, bf16[1024,128]{1,0:T(8,128)(2,1)} %collective-permute-done.refs_1_, bf16[1024,128]{1,0:T(8,128)(2,1)S(1)} %collective-permute-done.10.refs_2_.refs_1_), custom_call_target="tpu_custom_call" | custom-call | flops 1000 | bytes 1000 | tf_op jit(solution)/shard_map/pallas_call | solution.py:90
  42.6 0.1 collective-permute-start.11
  42.7 5.8 %collective-permute-done.4.refs_0_ = bf16[256,768]{1,0:T(8,128)(2,1)S(1)} collective-permute-done((bf16[256,768]{1,0:T(8,128)(2,1)S(1)}, bf16[256,768]{1,0:T(8,128)(2,1)S(1)}, u32[]{:S(2)}, u32[]{:S(2)}) %collective-permute-start.4) | collective-permute-done | bytes 393248 | tf_op jit(solution)/shard_map/ppermute | solution.py:44
  48.5 1.5 %collective-permute-start.5 = (bf16[1024,128]{1,0:T(8,128)(2,1)}, bf16[1024,128]{1,0:T(8,128)(2,1)S(1)}, u32[]{:S(2)}, u32[]{:S(2)}) collective-permute-start(bf16[1024,128]{1,0:T(8,128)(2,1)} %collective-permute-done.refs_1_), channel_id=1, source_target_pairs={{0,2},{1,3},{2,0},{3,1},{4,6},{5,7},{6,4},{7,5},{8,10},{9,11},{10,... | collective-permute-start | bytes 786440 | tf_op jit(solution)/shard_map/ppermute | solution.py:50
  50.0 3.3 %shard_map.59 = (f32[3,256,768]{2,1,0:T(8,128)S(1)}, bf16[3,512,768]{2,1,0:T(8,128)(2,1)S(1)}) custom-call(bf16[256,768]{1,0:T(8,128)(2,1)} %bitcast.refs_0_, bf16[256,768]{1,0:T(8,128)(2,1)} %collective-permute-done.2.refs_1_, bf16[256,768]{1,0:T(8,128)(2,1)S(1)} %collective-permute-done.3.refs_2_, bf16[256,768]{1,0:T(8,128)(2,1)S(1)} %collective-permute-done.8.refs_3_, ...), custom_call_target="tpu_custom_call" | custom-call | flops 1000 | bytes 10501000 | tf_op jit(solution)/shard_map/pallas_call | solution.py:90
  53.4 0.0 collective-permute-done.14.refs_7_
  53.4 1.7 %shard_map.60 = (bf16[4,256,256]{2,1,0:T(8,128)(2,1)S(1)}, bf16[4,16,128]{2,1,0:T(8,128)(2,1)S(1)}, bf16[2,256,512]{2,1,0:T(8,128)(2,1)S(1)}, bf16[2,256,512]{2,...) custom-call(bf16[256,768]{1,0:T(8,128)(2,1)S(1)} %collective-permute-done.4.refs_0_, ...), custom_call_target="tpu_custom_call" | custom-call | flops 1000 | bytes 17501000 | tf_op jit(solution)/shard_map/pallas_call | solution.py:90
  55.1 0.3 collective-permute-start.15
  55.4 0.3 collective-permute-start.16
  55.7 1.7 %collective-permute-done.5 = bf16[1024,128]{1,0:T(8,128)(2,1)S(1)} collective-permute-done((bf16[1024,128]{1,0:T(8,128)(2,1)}, bf16[1024,128]{1,0:T(8,128)(2,1)S(1)}, u32[]{:S(2)}, u32[]{:S(2)}) %collective-permute-start.5) | collective-permute-done | bytes 262176 | tf_op jit(solution)/shard_map/ppermute | solution.py:50
  57.5 1.6 %collective-permute-start.23 = (bf16[2,1024,128]{2,1,0:T(8,128)(2,1)S(1)}, bf16[2,1024,128]{2,1,0:T(8,128)(2,1)S(1)}, u32[]{:S(2)}, u32[]{:S(2)}) collective-permute-start(bf16[2,1024,128]{2,1,0:T(8,128)(2,1)S(1)} %shard_map.63), channel_id=1, source_target_pairs={{0,2},{1,3},{2,0},{3,1},{4,6},{5,7},{6,4},{7,5},{8,10},{9,11},{10,... | collective-permute-start | bytes 1572872 | tf_op jit(solution)/shard_map/ppermute | solution.py:50
  59.1 0.7 collective-permute-start.17
  59.8 0.7 collective-permute-start.18
  60.4 1.4 %collective-permute-start.26 = (bf16[1024,128]{1,0:T(8,128)(2,1)S(1)}, bf16[1024,128]{1,0:T(8,128)(2,1)S(1)}, u32[]{:S(2)}, u32[]{:S(2)}) collective-permute-start(bf16[1024,128]{1,0:T(8,128)(2,1)S(1)} %collective-permute-done.5), channel_id=1, source_target_pairs={{0,16},{1,17},{2,18},{3,19},{4,20},{5,21},{6,22},{7,23},{8,24},{9,... | collective-permute-start | bytes 786440 | tf_op jit(solution)/shard_map/ppermute | solution.py:56
  61.8 2.6 %shard_map.61 = (bf16[256,256]{1,0:T(8,128)(2,1)S(1)}, bf16[256,256]{1,0:T(8,128)(2,1)S(1)}) custom-call(s32[32]{0:T(128)S(1)} %copy-done.3, bf16[4,256,256]{2,1,0:T(8,128)(2,1)S(1)} %get-tuple-element.46.q.refs_3_, bf16[4,16,128]{2,1,0:T(8,128)(2,1)S(1)} %get-tuple-element.47.marks.refs_4_, bf16[2,256,512]{2,1,0:T(8,128)(2,1)S(1)} %get-tuple-element.48.kv.refs_5_, ...), custom_call_target="tpu_custom_call" | custom-call | flops 1000 | bytes 14001000 | tf_op jit(solution)/shard_map/pallas_call | solution.py:90
  64.5 6.5 %collective-permute-start.25 = (bf16[1024,128]{1,0:T(8,128)(2,1)S(1)}, bf16[1024,128]{1,0:T(8,128)(2,1)S(1)}, u32[]{:S(2)}, u32[]{:S(2)}) collective-permute-start(bf16[1024,128]{1,0:T(8,128)(2,1)S(1)} %collective-permute-done.10.refs_2_.refs_1_), channel_id=1, source_target_pairs={{0,8},{1,9},{2,10},{3,11},{8,12},{9,13},{10,14},{11,15},{12,4},{13... | collective-permute-start | bytes 786440 | tf_op jit(solution)/shard_map/ppermute | solution.py:44
  70.9 2.7 %shard_map.62 = (bf16[256,256]{1,0:T(8,128)(2,1)S(1)}, bf16[256,256]{1,0:T(8,128)(2,1)S(1)}, bf16[256,256]{1,0:T(8,128)(2,1)S(1)}, bf16[256,256]{1,0:T(8,128)(2,1)S(1)}) custom-call(bf16[256,256]{1,0:T(8,128)(2,1)S(1)} %get-tuple-element.50.refs_0_, bf16[256,256]{1,0:T(8,128)(2,1)S(1)} %get-tuple-element.51.refs_1_, s32[32]{0:T(128)S(1)} %copy-done.3, ...), custom_call_target="tpu_custom_call" | custom-call | flops 1000 | bytes 14001000 | tf_op jit(solution)/shard_map/pallas_call | solution.py:90
  73.6 0.7 collective-permute-start.19
  74.3 1.3 %collective-permute-start.20 = (bf16[256,256]{1,0:T(8,128)(2,1)S(1)}, bf16[256,256]{1,0:T(8,128)(2,1)S(1)}, u32[]{:S(2)}, u32[]{:S(2)}) collective-permute-start(bf16[256,256]{1,0:T(8,128)(2,1)S(1)} %get-tuple-element.55), channel_id=1, source_target_pairs={{0,16},{1,17},{2,18},{3,19},{4,20},{5,21},{6,22},{7,23},{8,24},{9,... | collective-permute-start | bytes 393224 | tf_op jit(solution)/shard_map/ppermute | solution.py:56
  75.7 1.5 %collective-permute-start.21 = (bf16[256,256]{1,0:T(8,128)(2,1)S(1)}, bf16[256,256]{1,0:T(8,128)(2,1)S(1)}, u32[]{:S(2)}, u32[]{:S(2)}) collective-permute-start(bf16[256,256]{1,0:T(8,128)(2,1)S(1)} %get-tuple-element.56), channel_id=1, source_target_pairs={{0,2},{1,3},{2,0},{3,1},{4,6},{5,7},{6,4},{7,5},{8,10},{9,11},{10,... | collective-permute-start | bytes 393224 | tf_op jit(solution)/shard_map/ppermute | solution.py:50
  77.2 0.6 collective-permute-done.25.refs_0_
  77.8 3.1 %collective-permute-done.19.refs_0_ = bf16[256,256]{1,0:T(8,128)(2,1)S(1)} collective-permute-done((bf16[256,256]{1,0:T(8,128)(2,1)S(1)}, bf16[256,256]{1,0:T(8,128)(2,1)S(1)}, u32[]{:S(2)}, u32[]{:S(2)}) %collective-permute-start.19) | collective-permute-done | bytes 131104 | tf_op jit(solution)/shard_map/ppermute | solution.py:56
  80.9 1.5 %collective-permute-done.20.refs_1_ = bf16[256,256]{1,0:T(8,128)(2,1)S(1)} collective-permute-done((bf16[256,256]{1,0:T(8,128)(2,1)S(1)}, bf16[256,256]{1,0:T(8,128)(2,1)S(1)}, u32[]{:S(2)}, u32[]{:S(2)}) %collective-permute-start.20) | collective-permute-done | bytes 131104 | tf_op jit(solution)/shard_map/ppermute | solution.py:56
  82.3 0.9 %collective-permute-done.21.refs_2_ = bf16[256,256]{1,0:T(8,128)(2,1)S(1)} collective-permute-done((bf16[256,256]{1,0:T(8,128)(2,1)S(1)}, bf16[256,256]{1,0:T(8,128)(2,1)S(1)}, u32[]{:S(2)}, u32[]{:S(2)}) %collective-permute-start.21) | collective-permute-done | bytes 131104 | tf_op jit(solution)/shard_map/ppermute | solution.py:50
  83.3 0.0 collective-permute-start.27
  83.3 1.9 %collective-permute-done.27.refs_11_ = bf16[2,1024,128]{2,1,0:T(8,128)(2,1)S(1)} collective-permute-done((bf16[2,1024,128]{2,1,0:T(8,128)(2,1)S(1)}, bf16[2,1024,128]{2,1,0:T(8,128)(2,1)S(1)}, u32[]{:S(2)}, u32[]{:S(2)}) %collective-permute-start.27) | collective-permute-done | bytes 524320 | tf_op jit(solution)/shard_map/ppermute | solution.py:50
  85.2 2.1 %shard_map.65 = bf16[256,2048]{1,0:T(8,128)(2,1)} custom-call(bf16[256,256]{1,0:T(8,128)(2,1)S(1)} %collective-permute-done.19.refs_0_, bf16[256,256]{1,0:T(8,128)(2,1)S(1)} %collective-permute-done.20.refs_1_, bf16[256,256]{1,0:T(8,128)(2,1)S(1)} %collective-permute-done.21.refs_2_, bf16[256,256]{1,0:T(8,128)(2,1)S(1)} %get-tuple-element.57.refs_3_, ...), custom_call_target="tpu_custom_call" | custom-call | flops 1000 | bytes 3501000 | tf_op jit(solution)/shard_map/pallas_call | solution.py:90
  (30 shorter events, 0.1 us)
Async XLA Ops:
  0.0 1.1 %copy-start.2 = (bf16[128,3072]{1,0:T(8,128)(2,1)S(1)}, bf16[128,3072]{1,0:T(8,128)(2,1)}, u32[]{:S(2)}) copy-start(bf16[128,3072]{1,0:T(8,128)(2,1)} %w.1) | copy-start | bytes 2359300
  1.3 11.2 %collective-permute-start = (bf16[1024,128]{1,0:T(8,128)(2,1)}, bf16[1024,128]{1,0:T(8,128)(2,1)}, u32[]{:S(2)}, u32[]{:S(2)}) collective-permute-start(bf16[1024,128]{1,0:T(8,128)(2,1)} %refs_0_.2), channel_id=1, source_target_pairs={{0,8},{1,9},{2,10},{3,11},{8,12},{9,13},{10,14},{11,15},{12,4},{13... | collective-permute-start | bytes 786440 | tf_op jit(solution)/shard_map/ppermute | solution.py:44
  5.4 6.4 %collective-permute-start.1 = (bf16[128,768]{1,0:T(8,128)(2,1)S(1)}, bf16[128,768]{1,0:T(8,128)(2,1)S(1)}, u32[]{:S(2)}, u32[]{:S(2)}) collective-permute-start(bf16[128,768]{1,0:T(8,128)(2,1)S(1)} %get-tuple-element.34), channel_id=1, source_target_pairs={{0,2},{1,3},{2,0},{3,1},{4,6},{5,7},{6,4},{7,5},{8,10},{9,11},{10,... | collective-permute-start | bytes 589832 | tf_op jit(solution)/shard_map/ppermute | solution.py:50
  6.9 1.2 %copy-start = (bf16[256,2048]{1,0:T(8,128)(2,1)S(1)}, bf16[256,2048]{1,0:T(8,128)(2,1)}, u32[]{:S(2)}) copy-start(bf16[256,2048]{1,0:T(8,128)(2,1)} %x) | copy-start | bytes 3145732
  8.1 0.7 copy-start.4
  9.4 25.8 %collective-permute-start.13 = (bf16[272,2048]{1,0:T(8,128)(2,1)S(1)}, bf16[272,2048]{1,0:T(8,128)(2,1)S(1)}, u32[]{:S(2)}, u32[]{:S(2)}) collective-permute-start(bf16[272,2048]{1,0:T(8,128)(2,1)S(1)} %shard_map.58.refs_6_.refs_4_), channel_id=1, source_target_pairs={{0,16},{1,17},{2,18},{3,19},{4,20},{5,21},{6,22},{7,23},{8,24},{9,... | collective-permute-start | bytes 3342344 | tf_op jit(solution)/shard_map/ppermute | solution.py:56
  12.5 25.2 %collective-permute-start.12 = (bf16[272,2048]{1,0:T(8,128)(2,1)S(1)}, bf16[272,2048]{1,0:T(8,128)(2,1)S(1)}, u32[]{:S(2)}, u32[]{:S(2)}) collective-permute-start(bf16[272,2048]{1,0:T(8,128)(2,1)S(1)} %shard_map.58.refs_6_.refs_4_), channel_id=1, source_target_pairs={{0,2},{1,3},{2,0},{3,1},{4,6},{5,7},{6,4},{7,5},{8,10},{9,11},{10,... | collective-permute-start | bytes 3342344 | tf_op jit(solution)/shard_map/ppermute | solution.py:50
  14.0 12.4 %collective-permute-start.2 = (bf16[256,768]{1,0:T(8,128)(2,1)}, bf16[256,768]{1,0:T(8,128)(2,1)}, u32[]{:S(2)}, u32[]{:S(2)}) collective-permute-start(bf16[256,768]{1,0:T(8,128)(2,1)} %bitcast.refs_0_), channel_id=1, source_target_pairs={{0,8},{1,9},{2,10},{3,11},{8,12},{9,13},{10,14},{11,15},{12,4},{13... | collective-permute-start | bytes 1179656 | tf_op jit(solution)/shard_map/ppermute | solution.py:44
  16.1 25.5 %copy-start.1 = (bf16[1024,128]{1,0:T(8,128)(2,1)S(1)}, bf16[1024,128]{1,0:T(8,128)(2,1)}, u32[]{:S(2)}) copy-start(bf16[1024,128]{1,0:T(8,128)(2,1)} %refs_0_.2) | copy-start | bytes 786436
  16.1 21.7 %collective-permute-start.8 = (bf16[256,768]{1,0:T(8,128)(2,1)}, bf16[256,768]{1,0:T(8,128)(2,1)S(1)}, u32[]{:S(2)}, u32[]{:S(2)}) collective-permute-start(bf16[256,768]{1,0:T(8,128)(2,1)} %bitcast.refs_0_), channel_id=1, source_target_pairs={{0,1},{1,0},{2,3},{3,2},{4,5},{5,4},{6,7},{7,6},{8,9},{9,8},{10,11... | collective-permute-start | bytes 1179656 | tf_op jit(solution)/shard_map/ppermute | solution.py:50
  16.1 21.7 %collective-permute-start.10 = (bf16[1024,128]{1,0:T(8,128)(2,1)}, bf16[1024,128]{1,0:T(8,128)(2,1)S(1)}, u32[]{:S(2)}, u32[]{:S(2)}) collective-permute-start(bf16[1024,128]{1,0:T(8,128)(2,1)} %collective-permute-done.refs_1_), channel_id=1, source_target_pairs={{0,8},{1,9},{2,10},{3,11},{8,12},{9,13},{10,14},{11,15},{12,4},{13... | collective-permute-start | bytes 786440 | tf_op jit(solution)/shard_map/ppermute | solution.py:44
  26.4 11.5 %collective-permute-start.3 = (bf16[256,768]{1,0:T(8,128)(2,1)}, bf16[256,768]{1,0:T(8,128)(2,1)S(1)}, u32[]{:S(2)}, u32[]{:S(2)}) collective-permute-start(bf16[256,768]{1,0:T(8,128)(2,1)} %collective-permute-done.2.refs_1_), channel_id=1, source_target_pairs={{0,8},{1,9},{2,10},{3,11},{8,12},{9,13},{10,14},{11,15},{12,4},{13... | collective-permute-start | bytes 1179656 | tf_op jit(solution)/shard_map/ppermute | solution.py:44
  35.2 2.7 %collective-permute-start.9 = (bf16[256,768]{1,0:T(8,128)(2,1)}, bf16[256,768]{1,0:T(8,128)(2,1)S(1)}, u32[]{:S(2)}, u32[]{:S(2)}) collective-permute-start(bf16[256,768]{1,0:T(8,128)(2,1)} %collective-permute-done.2.refs_1_), channel_id=1, source_target_pairs={{0,1},{1,0},{2,3},{3,2},{4,5},{5,4},{6,7},{7,6},{8,9},{9,8},{10,11... | collective-permute-start | bytes 1179656 | tf_op jit(solution)/shard_map/ppermute | solution.py:50
  37.9 15.6 %collective-permute-start.14 = (bf16[272,2048]{1,0:T(8,128)(2,1)S(1)}, bf16[272,2048]{1,0:T(8,128)(2,1)S(1)}, u32[]{:S(2)}, u32[]{:S(2)}) collective-permute-start(bf16[272,2048]{1,0:T(8,128)(2,1)S(1)} %broadcast_select_fusion), channel_id=1, source_target_pairs={{0,16},{1,3},{2,18},{3,1},{4,20},{5,7},{6,22},{7,5},{8,24},{9,11},... | collective-permute-start | bytes 3342344 | tf_op jit(solution)/shard_map/ppermute | solution.py:66
  39.5 9.0 %collective-permute-start.4 = (bf16[256,768]{1,0:T(8,128)(2,1)S(1)}, bf16[256,768]{1,0:T(8,128)(2,1)S(1)}, u32[]{:S(2)}, u32[]{:S(2)}) collective-permute-start(bf16[256,768]{1,0:T(8,128)(2,1)S(1)} %collective-permute-done.3.refs_2_), channel_id=1, source_target_pairs={{0,8},{1,9},{2,10},{3,11},{8,12},{9,13},{10,14},{11,15},{12,4},{13... | collective-permute-start | bytes 1179656 | tf_op jit(solution)/shard_map/ppermute | solution.py:44
  42.6 7.4 %collective-permute-start.11 = (bf16[256,768]{1,0:T(8,128)(2,1)S(1)}, bf16[256,768]{1,0:T(8,128)(2,1)S(1)}, u32[]{:S(2)}, u32[]{:S(2)}) collective-permute-start(bf16[256,768]{1,0:T(8,128)(2,1)S(1)} %collective-permute-done.3.refs_2_), channel_id=1, source_target_pairs={{0,1},{1,0},{2,3},{3,2},{4,5},{5,4},{6,7},{7,6},{8,9},{9,8},{10,11... | collective-permute-start | bytes 1179656 | tf_op jit(solution)/shard_map/ppermute | solution.py:50
  48.5 4.9 %collective-permute-start.7 = (bf16[256,768]{1,0:T(8,128)(2,1)S(1)}, bf16[256,768]{1,0:T(8,128)(2,1)S(1)}, u32[]{:S(2)}, u32[]{:S(2)}) collective-permute-start(bf16[256,768]{1,0:T(8,128)(2,1)S(1)} %collective-permute-done.4.refs_0_), channel_id=1, source_target_pairs={{0,1},{1,0},{2,3},{3,2},{4,5},{5,4},{6,7},{7,6},{8,9},{9,8},{10,11... | collective-permute-start | bytes 1179656 | tf_op jit(solution)/shard_map/ppermute | solution.py:50
  48.5 8.9 %collective-permute-start.5 = (bf16[1024,128]{1,0:T(8,128)(2,1)}, bf16[1024,128]{1,0:T(8,128)(2,1)S(1)}, u32[]{:S(2)}, u32[]{:S(2)}) collective-permute-start(bf16[1024,128]{1,0:T(8,128)(2,1)} %collective-permute-done.refs_1_), channel_id=1, source_target_pairs={{0,2},{1,3},{2,0},{3,1},{4,6},{5,7},{6,4},{7,5},{8,10},{9,11},{10,... | collective-permute-start | bytes 786440 | tf_op jit(solution)/shard_map/ppermute | solution.py:50
  53.4 8.4 %copy-start.3 = (s32[32]{0:T(128)S(1)}, s32[32]{0:T(128)}, u32[]{:S(2)}) copy-start(s32[32]{0:T(128)} %refs_2_.1) | copy-start | bytes 388
  55.1 5.3 %collective-permute-start.15 = (bf16[2,256,512]{2,1,0:T(8,128)(2,1)S(1)}, bf16[2,256,512]{2,1,0:T(8,128)(2,1)S(1)}, u32[]{:S(2)}, u32[]{:S(2)}) collective-permute-start(bf16[2,256,512]{2,1,0:T(8,128)(2,1)S(1)} %get-tuple-element.48.kv.refs_5_), channel_id=1, source_target_pairs={{0,1},{1,0},{2,3},{3,2},{4,5},{5,4},{6,7},{7,6},{8,9},{9,8},{10,11... | collective-permute-start | bytes 1572872 | tf_op jit(solution)/shard_map/ppermute | solution.py:50
  55.4 6.4 %collective-permute-start.16 = (bf16[2,256,512]{2,1,0:T(8,128)(2,1)S(1)}, bf16[2,256,512]{2,1,0:T(8,128)(2,1)S(1)}, u32[]{:S(2)}, u32[]{:S(2)}) collective-permute-start(bf16[2,256,512]{2,1,0:T(8,128)(2,1)S(1)} %get-tuple-element.49.kv_across.refs_6_), channel_id=1, source_target_pairs={{0,1},{1,0},{2,3},{3,2},{4,5},{5,4},{6,7},{7,6},{8,9},{9,8},{10,11... | collective-permute-start | bytes 1572872 | tf_op jit(solution)/shard_map/ppermute | solution.py:50
  57.4 2.3 %collective-permute-start.6 = (bf16[1024,128]{1,0:T(8,128)(2,1)S(1)}, bf16[1024,128]{1,0:T(8,128)(2,1)S(1)}, u32[]{:S(2)}, u32[]{:S(2)}) collective-permute-start(bf16[1024,128]{1,0:T(8,128)(2,1)S(1)} %collective-permute-done.5), channel_id=1, source_target_pairs={{0,1},{1,0},{2,3},{3,2},{4,5},{5,4},{6,7},{7,6},{8,9},{9,8},{10,11... | collective-permute-start | bytes 786440 | tf_op jit(solution)/shard_map/ppermute | solution.py:50
  57.5 18.2 %collective-permute-start.23 = (bf16[2,1024,128]{2,1,0:T(8,128)(2,1)S(1)}, bf16[2,1024,128]{2,1,0:T(8,128)(2,1)S(1)}, u32[]{:S(2)}, u32[]{:S(2)}) collective-permute-start(bf16[2,1024,128]{2,1,0:T(8,128)(2,1)S(1)} %shard_map.63), channel_id=1, source_target_pairs={{0,2},{1,3},{2,0},{3,1},{4,6},{5,7},{6,4},{7,5},{8,10},{9,11},{10,... | collective-permute-start | bytes 1572872 | tf_op jit(solution)/shard_map/ppermute | solution.py:50
  59.1 11.9 %collective-permute-start.17 = (bf16[256,512]{1,0:T(8,128)(2,1)S(1)}, bf16[256,512]{1,0:T(8,128)(2,1)S(1)}, u32[]{:S(2)}, u32[]{:S(2)}) collective-permute-start(bf16[256,512]{1,0:T(8,128)(2,1)S(1)} %get-tuple-element.52), channel_id=1, source_target_pairs={{1,4},{3,6},{4,1},{5,8},{6,3},{7,10},{8,5},{9,12},{10,7},{11,14},{... | collective-permute-start | bytes 786440 | tf_op jit(solution)/shard_map/ppermute | solution.py:72
  59.8 11.2 %collective-permute-start.18 = (bf16[256,512]{1,0:T(8,128)(2,1)S(1)}, bf16[256,512]{1,0:T(8,128)(2,1)S(1)}, u32[]{:S(2)}, u32[]{:S(2)}) collective-permute-start(bf16[256,512]{1,0:T(8,128)(2,1)S(1)} %get-tuple-element.53), channel_id=1, source_target_pairs={{1,4},{3,6},{4,1},{5,8},{6,3},{7,10},{8,5},{9,12},{10,7},{11,14},{... | collective-permute-start | bytes 786440 | tf_op jit(solution)/shard_map/ppermute | solution.py:72
  60.4 13.9 %collective-permute-start.26 = (bf16[1024,128]{1,0:T(8,128)(2,1)S(1)}, bf16[1024,128]{1,0:T(8,128)(2,1)S(1)}, u32[]{:S(2)}, u32[]{:S(2)}) collective-permute-start(bf16[1024,128]{1,0:T(8,128)(2,1)S(1)} %collective-permute-done.5), channel_id=1, source_target_pairs={{0,16},{1,17},{2,18},{3,19},{4,20},{5,21},{6,22},{7,23},{8,24},{9,... | collective-permute-start | bytes 786440 | tf_op jit(solution)/shard_map/ppermute | solution.py:56
  64.5 13.3 %collective-permute-start.25 = (bf16[1024,128]{1,0:T(8,128)(2,1)S(1)}, bf16[1024,128]{1,0:T(8,128)(2,1)S(1)}, u32[]{:S(2)}, u32[]{:S(2)}) collective-permute-start(bf16[1024,128]{1,0:T(8,128)(2,1)S(1)} %collective-permute-done.10.refs_2_.refs_1_), channel_id=1, source_target_pairs={{0,8},{1,9},{2,10},{3,11},{8,12},{9,13},{10,14},{11,15},{12,4},{13... | collective-permute-start | bytes 786440 | tf_op jit(solution)/shard_map/ppermute | solution.py:44
  70.9 14.3 %collective-permute-start.22 = (bf16[3,1024,128]{2,1,0:T(8,128)(2,1)S(1)}, bf16[3,1024,128]{2,1,0:T(8,128)(2,1)S(1)}, u32[]{:S(2)}, u32[]{:S(2)}) collective-permute-start(bf16[3,1024,128]{2,1,0:T(8,128)(2,1)S(1)} %shard_map.57.refs_4_), channel_id=1, source_target_pairs={{0,1},{1,0},{2,3},{3,2},{4,5},{5,4},{6,7},{7,6},{8,9},{9,8},{10,11... | collective-permute-start | bytes 2359304 | tf_op jit(solution)/shard_map/ppermute | solution.py:50
  73.6 7.3 %collective-permute-start.19 = (bf16[256,256]{1,0:T(8,128)(2,1)S(1)}, bf16[256,256]{1,0:T(8,128)(2,1)S(1)}, u32[]{:S(2)}, u32[]{:S(2)}) collective-permute-start(bf16[256,256]{1,0:T(8,128)(2,1)S(1)} %get-tuple-element.54), channel_id=1, source_target_pairs={{0,18},{1,19},{2,16},{3,17},{4,22},{5,23},{6,20},{7,21},{8,26},{9,... | collective-permute-start | bytes 393224 | tf_op jit(solution)/shard_map/ppermute | solution.py:56
  74.3 8.0 %collective-permute-start.20 = (bf16[256,256]{1,0:T(8,128)(2,1)S(1)}, bf16[256,256]{1,0:T(8,128)(2,1)S(1)}, u32[]{:S(2)}, u32[]{:S(2)}) collective-permute-start(bf16[256,256]{1,0:T(8,128)(2,1)S(1)} %get-tuple-element.55), channel_id=1, source_target_pairs={{0,16},{1,17},{2,18},{3,19},{4,20},{5,21},{6,22},{7,23},{8,24},{9,... | collective-permute-start | bytes 393224 | tf_op jit(solution)/shard_map/ppermute | solution.py:56
  75.7 7.6 %collective-permute-start.21 = (bf16[256,256]{1,0:T(8,128)(2,1)S(1)}, bf16[256,256]{1,0:T(8,128)(2,1)S(1)}, u32[]{:S(2)}, u32[]{:S(2)}) collective-permute-start(bf16[256,256]{1,0:T(8,128)(2,1)S(1)} %get-tuple-element.56), channel_id=1, source_target_pairs={{0,2},{1,3},{2,0},{3,1},{4,6},{5,7},{6,4},{7,5},{8,10},{9,11},{10,... | collective-permute-start | bytes 393224 | tf_op jit(solution)/shard_map/ppermute | solution.py:50
  77.8 5.5 %collective-permute-start.24 = (bf16[2,1024,128]{2,1,0:T(8,128)(2,1)S(1)}, bf16[2,1024,128]{2,1,0:T(8,128)(2,1)S(1)}, u32[]{:S(2)}, u32[]{:S(2)}) collective-permute-start(bf16[2,1024,128]{2,1,0:T(8,128)(2,1)S(1)} %collective-permute-done.23.refs_6_), channel_id=1, source_target_pairs={{0,1},{1,0},{2,3},{3,2},{4,5},{5,4},{6,7},{7,6},{8,9},{9,8},{10,11... | collective-permute-start | bytes 1572872 | tf_op jit(solution)/shard_map/ppermute | solution.py:50
  83.3 1.9 %collective-permute-start.27 = (bf16[2,1024,128]{2,1,0:T(8,128)(2,1)S(1)}, bf16[2,1024,128]{2,1,0:T(8,128)(2,1)S(1)}, u32[]{:S(2)}, u32[]{:S(2)}) collective-permute-start(bf16[2,1024,128]{2,1,0:T(8,128)(2,1)S(1)} %shard_map.64.refs_10_), channel_id=1, source_target_pairs={{0,1},{1,0},{2,3},{3,2},{4,5},{5,4},{6,7},{7,6},{8,9},{9,8},{10,11... | collective-permute-start | bytes 1572872 | tf_op jit(solution)/shard_map/ppermute | solution.py:50
